TPU v7x, 32 devices: a whole 2x2x4 slice. The times are simulated.
32 devices in a mesh: pts: 8 (over z, y), loc: 4 (over x, core).
Axes of the slice: x: 2, y: 2, z: 4, core: 2. Of those that a mesh axis runs over, the one named last changes fastest.
Arguments:
- points: bfloat16 [32768, 64], P(('pts', 'loc'))
- lengths: int32 [9], replicated, may hold values from 1024 to 8192, as said below
- neighbours_one: int32 [32768, 20], P(('pts', 'loc')), may hold values from 0 to 8191, as said below
- neighbours_two: int32 [32768, 20], P(('pts', 'loc')), may hold values from 0 to 8191, as said below
- weight_one: bfloat16 [128, 128], replicated, may hold values from -0.5 to 0.5
- gain_one: float32 [128], replicated, may hold values from 0.5 to 2
- shift_one: float32 [128], replicated, may hold values from -2.5 to 2.5
- weight_two: bfloat16 [256, 256], replicated, may hold values from -0.375 to 0.375
- gain_two: float32 [256], replicated, may hold values from 0.5 to 2
- shift_two: float32 [256], replicated, may hold values from -2.5 to 2.5
- cotangent: bfloat16 [32768, 256], P(('pts', 'loc')), may hold values from -6 to 6
Outputs:
- act_one: bfloat16 [32768, 128], P(('pts', 'loc'))
- act_two: bfloat16 [32768, 256], P(('pts', 'loc'))
- grad_points: float32 [32768, 64], P(('pts', 'loc'))
- grad_weight_one: float32 [128, 128], replicated
- grad_gain_one: float32 [128], replicated
- grad_shift_one: float32 [128], replicated
- grad_weight_two: float32 [256, 256], replicated
- grad_gain_two: float32 [256], replicated
- grad_shift_two: float32 [256], replicated
Inputs may be any that keep to these rules, and one draw needn't show every extreme that they name: `lengths`: exactly 3 lines of 8192 positions (b * 8192 to (b + 1) * 8192 - 1, which lines drawn from the seed) are each one cloud of 8192 points; each other line holds 6 clouds of 1024 points or more. No cloud crosses a line's end. `neighbours_one`: each entry is an index within the point's own cloud. For a point of a cloud that fills a line, the neighbours lie anywhere in the line, and of the 20480 entries of one device's points exactly 2560 fall on each device of that line; for a point of any other cloud every neighbour is stored on the point's own device. `neighbours_two`: as for neighbours_one, drawn independently.
All inputs are finite; a program needn't handle non-finite values.
Results may differ from a plain program's by a relative error of at most 0.009.
Values may be sent and summed in bfloat16 or wider, within the bound.
No kernel may reach another device: no remote copies, remote signals or barrier semaphores. Data moves between devices by JAX's collectives and lax.ppermute only.
A program may use at most 192 MiB of HBM per device.

v0:
```python
import functools
import math

import jax
import jax.numpy as jnp
from jax import lax
from jax.experimental import pallas as pl
from jax.experimental.pallas import tpu as pltpu
from jax.sharding import PartitionSpec as P

EPS = 1e-05
MIB = 1024 * 1024
BLOCK = 128
POOL_BLOCK = 256
GROUP = 8
LINES = 6
LINE_BYTES = 24 * MIB
POINTS = 32
ROWS = 16
AHEAD = 4
LOG2E = 1.0 / math.log(2.0)
LANES = 128
BOTH = ("pts", "loc")

f32 = jnp.float32
bf16 = jnp.bfloat16


def params():
    return pltpu.CompilerParams(vmem_limit_bytes=52 * MIB)


def lasting(microseconds):
    return pl.CostEstimate(flops=0, transcendentals=0, bytes_accessed=3_000_000 * microseconds)


def smem():
    return pl.BlockSpec(memory_space=pltpu.SMEM)


def fold_rows(x):
    return jnp.sum(x.reshape(x.shape[0] // 8, 8, x.shape[1]), axis=0)


def tree(op, terms):
    while len(terms) > 1:
        pairs = [op(a, b) for a, b in zip(terms[::2], terms[1::2])]
        terms = pairs + terms[len(pairs) * 2 :]
    return terms[0]


def dot(a, b):
    return jnp.dot(a, b, preferred_element_type=f32)


def exact(a, b):
    return jnp.dot(a, b, precision=lax.Precision.HIGHEST, preferred_element_type=f32)


def dot_t(a, b):
    return lax.dot_general(a, b, (((1,), (1,)), ((), ())), preferred_element_type=f32)


def edge_kernel(pieces, *refs):
    table_refs = refs[1 : 1 + pieces]
    idx_ref = refs[0]
    own_ref, w_ref, diff_ref, z_ref, stat_ref, pivot_ref, table, rows, centre, sums, square = refs[
        1 + pieces :
    ]
    near, block, c = diff_ref.shape
    step_id = pl.program_id(0)
    last = pl.num_programs(0) - 1
    chunk = 10

    def project(own_sum, diff_sum):
        weight = w_ref[...].astype(f32)
        both = exact(own_sum, weight[:c]) + exact(diff_sum, weight[c:])
        return jnp.sum(both, axis=0, keepdims=True)

    @pl.when(step_id == 0)
    def _():
        first = 0
        for piece in table_refs:
            for r in range(0, piece.shape[0], 256):
                table[pl.ds(first + r, 256), :c] = piece[pl.ds(r, 256), :].astype(f32)
            first += piece.shape[0]
        sums[...] = jnp.zeros_like(sums)
        square[...] = jnp.zeros_like(square)

    @pl.when(step_id == 1)
    def _():
        own = own_ref[...].astype(f32)
        diff_sum = jnp.zeros((8, c), f32)
        for k in range(near):
            diff_sum = diff_sum + fold_rows(rows[pl.ds(k * block, block), :c] - own)
        own_sum = fold_rows(own) * float(near)
        pivot_ref[...] = project(own_sum, diff_sum) * (1.0 / (near * block))

    def pick(k):
        base = pl.multiple_of(k * block, block)
        at = step_id * near + k
        waiting = []
        for e in range(block + GROUP):
            if e < block:
                waiting.append(table[pl.ds(idx_ref[at, e], 1), :])
            if e >= GROUP:
                rows[pl.ds(base + (e - GROUP), 1), :] = waiting[e - GROUP]

    def work(k, own, carry, between=lambda: None):
        diff_sum, total = carry
        at = pl.ds(pl.multiple_of(k * block, block), block)
        diff = (rows[at, :c] - own).astype(bf16)
        diff_ref[k] = diff
        diff_sum = diff_sum + fold_rows(diff.astype(f32))
        product = dot(diff, w_ref[c:, :])
        between()
        z = product + centre[...]
        z_ref[k] = z
        return diff_sum, total + fold_rows(z * z)

    @pl.when(step_id == 0)
    def _():
        def body(i, _):
            pick(i)
            return 0

        lax.fori_loop(0, near, body, 0)

    def finish(own, carry):
        sums[0] += fold_rows(own) * float(near)
        sums[1] += carry[0]
        square[...] += carry[1]

    def begin():
        centre[...] = dot(own_ref[...], w_ref[:c, :]) - pivot_ref[...]
        zero = (jnp.zeros((8, c), f32), jnp.zeros_like(square[...]))
        return own_ref[...].astype(f32), zero

    @pl.when((step_id > 0) & (step_id < last))
    def _():
        own, zero = begin()

        def body(i, carry):
            for k in range(chunk):
                at = i * chunk + k
                carry = work(at, own_ref[...].astype(f32), carry, functools.partial(pick, at))
            return carry

        finish(own, lax.fori_loop(0, near // chunk, body, zero))

    @pl.when(step_id == last)
    def _():
        own, carry = begin()
        for k in range(near):
            carry = work(k, own, carry)
        finish(own, carry)
        count = float(near * block * (pl.num_programs(0) - 1))
        mean = project(sums[0], sums[1]) / count
        off = mean - pivot_ref[...]
        m2 = jnp.sum(square[...], axis=0, keepdims=True) - count * off * off
        stat_ref[...] = jnp.broadcast_to(jnp.concatenate([mean, m2], axis=0)[None], stat_ref.shape)


def edge_stats(index, pieces, own, weight):
    rows, c = own.shape
    d = weight.shape[1]
    blocks = rows // BLOCK
    near = index.shape[0] // blocks
    total = sum(piece.shape[0] for piece in pieces)
    before = lambda b: jnp.maximum(b - 1, 0)
    whole = lambda x: pl.BlockSpec(x.shape, lambda b: (0,) * len(x.shape))
    stat = jax.ShapeDtypeStruct((lax.axis_size(BOTH), 2, d), f32)
    pivot = jax.ShapeDtypeStruct((1, d), f32)
    return pl.pallas_call(
        functools.partial(edge_kernel, len(pieces)),
        grid=(blocks + 1,),
        out_shape=(
            jax.ShapeDtypeStruct((near, rows, c), bf16),
            jax.ShapeDtypeStruct((near, rows, d), f32),
            stat,
            pivot,
        ),
        in_specs=[smem()]
        + [whole(piece) for piece in pieces]
        + [pl.BlockSpec((BLOCK, c), lambda b: (before(b), 0)), whole(weight)],
        out_specs=(
            pl.BlockSpec((near, BLOCK, c), lambda b: (0, before(b), 0)),
            pl.BlockSpec((near, BLOCK, d), lambda b: (0, before(b), 0)),
            whole(stat),
            whole(pivot),
        ),
        scratch_shapes=[
            pltpu.VMEM((total, LANES), f32),
            pltpu.VMEM((near * BLOCK, LANES), f32),
            pltpu.VMEM((BLOCK, d), f32),
            pltpu.VMEM((2, 8, c), f32),
            pltpu.VMEM((8, d), f32),
        ],
        compiler_params=params(),
        cost_estimate=lasting(22),
        name="edge_stats",
    )(index, *pieces, own, weight)


def moments(stat, edges_each):
    devices = stat.shape[0]
    means = stat[:, 0, :]
    mean = jnp.sum(means, axis=0, keepdims=True) * (1.0 / devices)
    off = means - mean
    m2 = jnp.sum(stat[:, 1, :], axis=0, keepdims=True) + edges_each * jnp.sum(
        off * off, axis=0, keepdims=True
    )
    return mean, lax.rsqrt(m2 * (1.0 / (edges_each * devices)) + EPS)


def pool_kernel(last, edges_each, z_ref, stat_ref, pivot_ref, norm_ref, *refs):
    near, block, d = z_ref.shape
    if last:
        cot_ref, pooled_ref, slope_ref, sums_ref, sums = refs
    else:
        pooled_ref, slope_ref, sum_ref, moment_ref = refs
    mean, inv = moments(stat_ref[...], edges_each)
    half_scale = norm_ref[0:1, :] * inv * 0.5
    half_offset = (pivot_ref[...] - mean) * half_scale + norm_ref[1:2, :] * 0.5
    if last:

        @pl.when(pl.program_id(0) == 0)
        def _():
            sums[...] = jnp.zeros_like(sums)

    for lane in range(0, d, 128):
        lanes = pl.ds(lane, 128)
        scale = jnp.broadcast_to(half_scale[:, lane : lane + 128], (ROWS, 128))
        offset = jnp.broadcast_to(half_offset[:, lane : lane + 128], (ROWS, 128))

        def step(b, carry, lanes=lanes, scale=scale, offset=offset):
            at = pl.ds(pl.multiple_of(b * ROWS, ROWS), ROWS)
            active, bends = [], []
            for k in range(near):
                half = z_ref[k, at, lanes] * scale + offset
                bent = jnp.tanh(half)
                t = 1.0 + bent
                a = half * t
                active.append(a)
                bends.append(t + a * (1.0 - bent))
            top = tree(jnp.maximum, active)
            powers = [jnp.exp2((a - top) * LOG2E) for a in active]
            total = tree(jnp.add, powers)
            pooled = top + jnp.log(total) - math.log(near)
            pooled_ref[at, lanes] = pooled.astype(bf16)
            factor = 0.5 / total
            if last:
                factor = factor * cot_ref[at, lanes].astype(f32)
            halves = [z_ref[k, at, lanes] * scale + offset for k in range(near)]
            slopes = [(powers[k] * factor) * bends[k] for k in range(near)]
            slope_sum = tree(jnp.add, slopes)
            slope_moment = tree(jnp.add, [slopes[k] * halves[k] for k in range(near)])
            for k in range(near):
                slope_ref[k, at, lanes] = slopes[k]
            if not last:
                sum_ref[at, lanes] = slope_sum
                moment_ref[at, lanes] = slope_moment
                return carry
            return (carry[0] + slope_sum, carry[1] + slope_moment)

        zero = jnp.zeros((ROWS, 128), f32)
        carry = lax.fori_loop(0, block // ROWS, step, (zero, zero))
        if last:
            sums[0:1, lanes] += jnp.sum(carry[0], axis=0, keepdims=True)
            sums[1:2, lanes] += jnp.sum(carry[1], axis=0, keepdims=True)
    if last:

        @pl.when(pl.program_id(0) == pl.num_programs(0) - 1)
        def _():
            sums_ref[...] = jnp.broadcast_to(sums[...][None], sums_ref.shape)


def pool(z, stat, pivot, norm, cot=None):
    near, rows, d = z.shape
    whole = lambda x: pl.BlockSpec(x.shape, lambda b: (0,) * len(x.shape))
    by_block = pl.BlockSpec((POOL_BLOCK, d), lambda b: (b, 0))
    by_edge = pl.BlockSpec((near, POOL_BLOCK, d), lambda b: (0, b, 0))
    inputs = [z, stat, pivot, norm]
    in_specs = [by_edge, whole(stat), whole(pivot), whole(norm)]
    row_out = lambda kind: (jax.ShapeDtypeStruct((rows, d), kind), by_block)
    outs = [row_out(bf16), (jax.ShapeDtypeStruct((near, rows, d), f32), by_edge)]
    scratch = []
    if cot is None:
        outs += [row_out(f32), row_out(f32)]
    else:
        inputs.append(cot)
        in_specs.append(by_block)
        sums = jax.ShapeDtypeStruct(stat.shape, f32)
        outs.append((sums, whole(sums)))
        scratch.append(pltpu.VMEM((2, d), f32))
    return pl.pallas_call(
        functools.partial(pool_kernel, cot is not None, float(near * rows)),
        grid=(rows // POOL_BLOCK,),
        out_shape=tuple(o[0] for o in outs),
        in_specs=in_specs,
        out_specs=tuple(o[1] for o in outs),
        scratch_shapes=scratch,
        compiler_params=params(),
        cost_estimate=lasting(12 if cot is None else 20),
        name="pool",
    )(*inputs)


def grads_kernel(
    edges_each,
    inner,
    turn_lines,
    idx_ref,
    slope_ref,
    z_ref,
    back_ref,
    stat_ref,
    pivot_ref,
    norm_ref,
    grads_ref,
    *refs,
):
    near, block, d = slope_ref.shape
    if inner:
        upstream_ref, diff_ref, line_ref, dz_sum_ref, weight_ref, send_ref = refs[: -turn_lines - 2]
    else:
        line_ref, dz_sum_ref, dz_ref, send_ref = refs[: -turn_lines - 2]
    fresh, held, *lines = refs[-turn_lines - 2 :]
    step_id = pl.program_id(0)
    last = pl.num_programs(0) - 1
    total, rows = lines[0].shape[0], dz_sum_ref.shape[0]
    turns = block // POINTS
    share = near * POINTS

    def store(waiting, most):
        while len(waiting) > most:
            line, place, row = waiting.pop(0)
            line[place, :] = row

    def add(turn, edges, waiting):
        for e in edges:
            line = lines[e % turn_lines]
            place = pl.ds(idx_ref[turn, e], 1)
            waiting.append((line, place, line[place, :] + held[pl.ds(e, 1), :]))
            store(waiting, turn_lines - 1)

    @pl.when(step_id == 0)
    def _():
        def clear(i, _):
            at = pl.ds(pl.multiple_of(i * 256, 256), 256)
            for line in lines:
                line[at, :] = jnp.zeros((256, LANES), f32)
            return 0

        lax.fori_loop(0, total // 256, clear, 0)
        fresh[...] = jnp.zeros_like(fresh)
        if inner:
            weight_ref[...] = jnp.zeros_like(weight_ref)

    edges = edges_each * stat_ref.shape[0]
    mean, inv = moments(stat_ref[...], edges_each)
    gain = norm_ref[0:1, :]
    sums = jnp.sum(grads_ref[...], axis=0)
    grad_shift = sums[0:1]
    grad_gain = (2.0 * sums[1:2] - norm_ref[1:2, :] * grad_shift) / gain
    alpha = gain * inv
    rate = alpha * inv * grad_gain * (1.0 / edges)
    constant = alpha * grad_shift * (1.0 / edges) + rate * (pivot_ref[...] - mean)
    wide = [
        [jnp.broadcast_to(x[:, lane : lane + 128], (POINTS, 128)) for x in (alpha, rate, constant)]
        for lane in range(0, d, 128)
    ]

    def turn(t, _):
        at = pl.ds(pl.multiple_of(t * POINTS, POINTS), POINTS)
        before = jnp.maximum(step_id * turns + t - 1, 0)
        held[...] = fresh[...]
        units = [(k, i) for i in range(d // 128) for k in range(near)]
        factors = [w[0] for w in wide]
        if inner:
            factors = [
                f * upstream_ref[at, pl.ds(i * 128, 128)] for i, f in enumerate(factors)
            ]

        def load(unit):
            k, i = unit
            lanes = pl.ds(i * 128, 128)
            return slope_ref[k, at, lanes], z_ref[k, at, lanes]

        loaded = [load(unit) for unit in units[:AHEAD]]
        dzs, waiting = {}, []
        each = share // 2 // len(units)
        for n, (k, i) in enumerate(units):
            add(before, range(n * each, (n + 1) * each), waiting)
            if n + AHEAD < len(units):
                loaded.append(load(units[n + AHEAD]))
            slope, z = loaded[n]
            dzs[k, i] = (factors[i] * slope - wide[i][2] - wide[i][1] * z).astype(bf16)
            if not inner:
                dz_ref[k, at, pl.ds(i * 128, 128)] = dzs[k, i]
        whole = [
            jnp.concatenate([dzs[k, i] for k in range(near)], axis=0) for i in range(d // 128)
        ]
        flat = jnp.concatenate(whole, axis=1)
        product = dot_t(flat, back_ref[...]).astype(bf16)
        if inner:
            weight_ref[...] += lax.dot_general(
                diff_ref[:, at, :].reshape(share, diff_ref.shape[2]),
                flat,
                (((0,), (0,)), ((), ())),
                preferred_element_type=f32,
            )
        add(before, range(share // 2, share), waiting)
        row = pl.multiple_of(step_id * block + t * POINTS, POINTS)
        for i in range(d // 128):
            dz_sum_ref[pl.ds(row, POINTS), pl.ds(i * 128, 128)] = tree(
                jnp.add, [dzs[k, i].astype(f32) for k in range(near)]
            )
        store(waiting, 0)
        fresh[...] = product.astype(f32)
        return 0

    lax.fori_loop(0, turns, turn, 0)
    @pl.when(step_id == last)
    def _():
        held[...] = fresh[...]
        waiting = []
        add(rows // POINTS - 1, range(share), waiting)
        store(waiting, 0)

        def join(i, _):
            at = pl.ds(pl.multiple_of(i * 256, 256), 256)
            joined = tree(jnp.add, [line[at, :] for line in lines])
            line_ref[at, :] = joined[:, : line_ref.shape[1]].astype(bf16)
            return 0

        lax.fori_loop(0, total // 256, join, 0)
        send_ref[...] = line_ref[pl.ds(total // 2, rows), :]


def edge_grads(turns, slope, z, weight, stat, pivot, norm, grads, total, inner=()):
    near, rows, d = slope.shape
    c = weight.shape[0] // 2
    whole = lambda x: pl.BlockSpec(x.shape, lambda b: (0,) * len(x.shape))
    by_block = lambda width: pl.BlockSpec((BLOCK, width), lambda b: (b, 0))
    by_edge = lambda width: pl.BlockSpec((near, BLOCK, width), lambda b: (0, b, 0))
    turn_lines = min(LINES, LINE_BYTES // (total * LANES * 4))
    back = jnp.pad(weight[c:], ((0, LANES - c), (0, 0)))
    inputs = [turns, slope, z, back, stat, pivot, norm, grads, *inner]
    in_specs = [
        smem(),
        by_edge(d),
        by_edge(d),
        whole(back),
        whole(stat),
        whole(pivot),
        whole(norm),
        whole(grads),
    ]
    if inner:
        in_specs += [by_block(d), by_edge(c)]
    dz = jax.ShapeDtypeStruct((near, rows, d), bf16)
    dz_sum = jax.ShapeDtypeStruct((rows, d), f32)
    line = jax.ShapeDtypeStruct((total, c), bf16)
    send = jax.ShapeDtypeStruct((rows, c), bf16)
    outs = [
        (line, whole(line)),
        (dz_sum, whole(dz_sum)),
    ]
    scratch = [
        pltpu.VMEM((near * POINTS, LANES), f32),
        pltpu.VMEM((near * POINTS, LANES), f32),
        *[pltpu.VMEM((total, LANES), f32)] * turn_lines,
    ]
    if inner:
        part = jax.ShapeDtypeStruct((c, d), f32)
        outs.append((part, whole(part)))
    else:
        outs.append((dz, by_edge(d)))
    outs.append((send, whole(send)))
    return pl.pallas_call(
        functools.partial(grads_kernel, float(near * rows), bool(inner), turn_lines),
        grid=(rows // BLOCK,),
        out_shape=tuple(o[0] for o in outs),
        in_specs=in_specs,
        out_specs=tuple(o[1] for o in outs),
        scratch_shapes=scratch,
        compiler_params=params(),
        cost_estimate=lasting(35),
        name="edge_grads",
    )(*inputs)


def copies(x):
    return jnp.broadcast_to(x[None], (lax.axis_size(BOTH),) + x.shape)


def shared(x):
    devices = lax.axis_size(BOTH)
    return x.reshape(devices, x.shape[0] // devices, x.shape[1])


def exchange(shares):
    return lax.all_to_all(shares, BOTH, split_axis=0, concat_axis=0, tiled=True)


def everyone(x):
    return exchange(copies(x))


def ring_moves(places):
    ring = list(range(0, places, 2)) + list(range(1, places, 2))[::-1]
    onward = [(ring[i], ring[(i + 1) % places]) for i in range(places)]
    return onward, [(b, a) for a, b in onward]


def ring_place(device, places):
    return jnp.where(device % 2 == 0, device // 2, places - 1 - device // 2)


def line_table(values):
    places = lax.axis_size("pts")
    onward, backward = ring_moves(places)
    rows, far = values.shape[0] // 2, places // 2
    behind, ahead = [values], [values]
    for _ in range(far - 1):
        behind.append(lax.ppermute(behind[-1], "pts", onward))
        ahead.append(lax.ppermute(ahead[-1], "pts", backward))
    farthest = [
        lax.ppermute(behind[-1][:rows], "pts", onward),
        lax.ppermute(ahead[-1][rows:], "pts", backward),
    ]
    return behind + farthest + ahead[:0:-1]


def owners_sum(line, send, centre, weights=None):
    places = lax.axis_size("pts")
    onward, backward = ring_moves(places)
    rows = centre.shape[0]
    half, far = rows // 2, places // 2

    def slot(j):
        return line[j * rows : (j + 1) * rows].astype(f32)

    forth = lax.ppermute(send[:half], "pts", onward)
    back = lax.ppermute(send[half:], "pts", backward)
    forth, back, centre = lax.optimization_barrier((forth, back, centre))
    if weights is not None:
        forth, back, weights = lax.optimization_barrier((forth, back, weights))
        shares = exchange(shared(weights))
    forth = jnp.pad(forth.astype(f32), ((0, half), (0, 0)))
    back = jnp.pad(back.astype(f32), ((half, 0), (0, 0)))
    for j in range(1, far):
        forth, back = (forth + slot(far + j)).astype(bf16), (back + slot(far - j)).astype(bf16)
        forth, back = lax.optimization_barrier((forth, back))
        if weights is not None and j == far - 1:
            forth, back, shares = lax.optimization_barrier((forth, back, shares))
            weights = everyone(jnp.sum(shares.astype(f32), axis=0).astype(bf16))
        forth = lax.ppermute(forth, "pts", onward).astype(f32)
        back = lax.ppermute(back, "pts", backward).astype(f32)
    return centre + slot(0) + forth + back, weights


def centre_grad(dz_sum, weight):
    wide = weight.astype(f32)
    c = weight.shape[0] // 2
    return exact(dz_sum, (wide[:c] - wide[c:]).T)


def per_device(
    points,
    lengths,
    neighbours_one,
    neighbours_two,
    weight_one,
    gain_one,
    shift_one,
    weight_two,
    gain_two,
    shift_two,
    cotangent,
):
    line_devices = lax.axis_size("pts")
    row_count = points.shape[0]
    line_length = line_devices * row_count
    table_one = line_table(points)

    norm_one, norm_two = jnp.stack([gain_one, shift_one]), jnp.stack([gain_two, shift_two])

    cloud_ends = jnp.cumsum(lengths)
    cloud_starts = cloud_ends - lengths
    line_first = lax.axis_index("loc") * line_length
    position = (
        line_first + lax.axis_index("pts") * row_count + jnp.arange(row_count, dtype=jnp.int32)
    )
    begins = (position[:, None] >= cloud_starts[None, :]) & (position[:, None] < cloud_ends[None, :])
    begin = jnp.sum(jnp.where(begins, cloud_starts[None, :], 0), axis=1) - line_first
    here = ring_place(lax.axis_index("pts"), line_devices)

    def slot_rows(neighbours):
        within = neighbours.T + begin[None, :]
        slot = (here - ring_place(within // row_count, line_devices)) % line_devices
        return slot * row_count + within % row_count

    def by_blocks(index, points):
        return index.reshape(index.shape[0], -1, points).transpose(1, 0, 2)

    index_one = slot_rows(neighbours_one)
    index_two = slot_rows(neighbours_two)
    order_one = by_blocks(index_one, BLOCK).reshape(-1, BLOCK)
    order_two = by_blocks(index_two, BLOCK).reshape(-1, BLOCK)
    turns_one = by_blocks(index_one, POINTS).reshape(row_count // POINTS, -1)
    turns_two = by_blocks(index_two, POINTS).reshape(row_count // POINTS, -1)

    diff_one, z_one, stat_one, pivot_one = edge_stats(order_one, table_one, points, weight_one)
    stat_one, order_two, turns_one, turns_two = lax.optimization_barrier(
        (exchange(stat_one), order_two, turns_one, turns_two)
    )
    act_one, slope_one, slope_sum, slope_moment = pool(z_one, stat_one, pivot_one, norm_one)
    table_two = line_table(act_one)
    diff_two, z_two, stat_two, pivot_two = edge_stats(order_two, table_two, act_one, weight_two)
    stat_two = exchange(stat_two)
    act_two, slope_two, sums_two = pool(z_two, stat_two, pivot_two, norm_two, cotangent)
    sums_two = exchange(sums_two)
    line_two, dz_sum_two, dz_two, send_two = edge_grads(
        turns_two,
        slope_two,
        z_two,
        weight_two,
        stat_two,
        pivot_two,
        norm_two,
        sums_two,
        line_length,
    )
    grad_first, _ = owners_sum(line_two, send_two, centre_grad(dz_sum_two, weight_two))
    grad_first, dz_two, dz_sum_two = lax.optimization_barrier((grad_first, dz_two, dz_sum_two))
    first_two = exact(act_one.astype(f32).T, dz_sum_two)
    second_two = jnp.einsum("kgc,kgd->cd", diff_two, dz_two, preferred_element_type=f32)
    sums_one = jnp.stack(
        [jnp.sum(grad_first * slope_sum, axis=0), jnp.sum(grad_first * slope_moment, axis=0)]
    )
    sums_one = everyone(sums_one)
    line_one, dz_sum_one, second_one, send_one = edge_grads(
        turns_one,
        slope_one,
        z_one,
        weight_one,
        stat_one,
        pivot_one,
        norm_one,
        sums_one,
        line_length,
        (grad_first, diff_one),
    )
    first_one = exact(points.astype(f32).T, dz_sum_one)
    weights = jnp.concatenate(
        [first_two.reshape(-1, LANES), second_two.reshape(-1, LANES), first_one, second_one], axis=0
    )
    grad_points, weights = owners_sum(
        line_one, send_one, centre_grad(dz_sum_one, weight_one), weights.astype(bf16)
    )
    weights = weights.reshape(-1, LANES).astype(f32)
    grad_weight_two = weights[: -weight_one.shape[0]].reshape(weight_two.shape)
    grad_weight_one = weights[-weight_one.shape[0] :]

    def norm_grads(sums, gain, shift):
        sums = jnp.sum(sums, axis=0)
        return (2.0 * sums[1] - shift * sums[0]) / gain, sums[0]

    grad_gain_one, grad_shift_one = norm_grads(sums_one, gain_one, shift_one)
    grad_gain_two, grad_shift_two = norm_grads(sums_two, gain_two, shift_two)
    return (
        act_one,
        act_two,
        grad_points,
        grad_weight_one,
        grad_gain_one,
        grad_shift_one,
        grad_weight_two,
        grad_gain_two,
        grad_shift_two,
    )


def solution(mesh):
    rows, copied = P(("pts", "loc"), None), P()
    in_specs = (rows, copied, rows, rows) + (copied,) * 6 + (rows,)
    out_specs = (rows, rows, rows) + (copied,) * 6
    return jax.shard_map(
        per_device, mesh=mesh, in_specs=in_specs, out_specs=out_specs, check_vma=False
    )
```

profile of v0, /device:TPU:1, one launch (start us, length us, event | category | flops | bytes accessed | tf_op | source)
XLA Modules:
  0.0 340.9 jit_solution(16480904040146308286)
XLA Ops:
  1.8 2.2 collective-permute-start
  5.4 4.5 %collective-permute-done.refs_2_ = bf16[1024,64]{1,0:T(8,128)(2,1)S(1)} collective-permute-done((bf16[1024,64]{1,0:T(8,128)(2,1)S(1)}, bf16[1024,64]{1,0:T(8,128)(2,1)S(1)}, u32[]{:S(2)}, u32[]{:S(2)}) %collective-permute-start) | collective-permute-done | bytes 131104 | tf_op jit(solution)/shard_map/ppermute | solution.py:527
  9.9 1.2 collective-permute-start.1
  11.5 5.0 %collective-permute-done.1.refs_3_ = bf16[1024,64]{1,0:T(8,128)(2,1)S(1)} collective-permute-done((bf16[1024,64]{1,0:T(8,128)(2,1)S(1)}, bf16[1024,64]{1,0:T(8,128)(2,1)S(1)}, u32[]{:S(2)}, u32[]{:S(2)}) %collective-permute-start.1) | collective-permute-done | bytes 131104 | tf_op jit(solution)/shard_map/ppermute | solution.py:527
  18.0 4.2 %collective-permute-done.2.refs_4_ = bf16[1024,64]{1,0:T(8,128)(2,1)S(1)} collective-permute-done((bf16[1024,64]{1,0:T(8,128)(2,1)S(1)}, bf16[1024,64]{1,0:T(8,128)(2,1)S(1)}, u32[]{:S(2)}, u32[]{:S(2)}) %collective-permute-start.2) | collective-permute-done | bytes 131104 | tf_op jit(solution)/shard_map/ppermute | solution.py:527
  24.9 1.4 fusion.13
  28.0 23.3 %edge_stats.2 = (bf16[20,1024,64]{2,1,0:T(8,128)(2,1)}, f32[20,1024,128]{2,1,0:T(8,128)}, f32[32,2,128]{2,1,0:T(2,128)}, f32[1,128]{1,0:T(1,128)S(1)}) custom-call(s32[160,128]{1,0:T(8,128)S(1)} %reshape.99.refs_0_, bf16[1024,64]{1,0:T(8,128)(2,1)S(1)} %copy.45.refs_1_.refs_10_, bf16[1024,64]{1,0:T(8,128)(2,1)S(1)} %collective-permute-done.refs_2_, ...), custom_call_target="tpu_custom_call" | custom-call | bytes 66000000 | tf_op jit(solution)/shard_map/edge_stats/pallas_call | solution.py:174
  51.3 9.6 %all-to-all-start = ((f32[32,2,128]{2,1,0:T(2,128)}), f32[32,2,128]{2,1,0:T(2,128)S(1)}, u32[]{:S(2)}, u32[]{:S(2)}) async-start(f32[32,2,128]{2,1,0:T(2,128)} %get-tuple-element.64), calls=%async_computation | async-start | bytes 65536 | tf_op jit(solution)/shard_map/all_to_all | solution.py:504
  61.0 7.1 %all-to-all-done.stat_ref = f32[32,2,128]{2,1,0:T(2,128)S(1)} async-done(((f32[32,2,128]{2,1,0:T(2,128)}), f32[32,2,128]{2,1,0:T(2,128)S(1)}, u32[]{:S(2)}, u32[]{:S(2)}) %all-to-all-start) | async-done | bytes 32800 | tf_op jit(solution)/shard_map/all_to_all | solution.py:504
  68.1 12.1 %pool.2 = (bf16[1024,128]{1,0:T(8,128)(2,1)}, f32[20,1024,128]{2,1,0:T(8,128)}, f32[1024,128]{1,0:T(8,128)S(1)}, f32[1024,128]{1,0:T(8,128)S(1)}) custom-call(f32[20,1024,128]{2,1,0:T(8,128)} %get-tuple-element.63.z_ref, f32[32,2,128]{2,1,0:T(2,128)S(1)} %all-to-all-done.stat_ref, f32[1,128]{1,0:T(1,128)S(1)} %get-tuple-element.66.pivot_ref, ...), custom_call_target="tpu_custom_call" | custom-call | bytes 36000000 | tf_op jit(solution)/shard_map/pool/pallas_call | solution.py:296
  80.2 1.5 collective-permute-start.12
  81.7 6.2 %collective-permute-done.8.refs_2_ = bf16[1024,128]{1,0:T(8,128)(2,1)S(1)} collective-permute-done((bf16[1024,128]{1,0:T(8,128)(2,1)}, bf16[1024,128]{1,0:T(8,128)(2,1)S(1)}, u32[]{:S(2)}, u32[]{:S(2)}) %collective-permute-start.8) | collective-permute-done | bytes 262176 | tf_op jit(solution)/shard_map/ppermute | solution.py:527
  87.9 1.5 collective-permute-start.13
  89.4 5.1 %collective-permute-done.9.refs_3_ = bf16[1024,128]{1,0:T(8,128)(2,1)S(1)} collective-permute-done((bf16[1024,128]{1,0:T(8,128)(2,1)S(1)}, bf16[1024,128]{1,0:T(8,128)(2,1)S(1)}, u32[]{:S(2)}, u32[]{:S(2)}) %collective-permute-start.9) | collective-permute-done | bytes 262176 | tf_op jit(solution)/shard_map/ppermute | solution.py:527
  94.5 1.5 collective-permute-start.14
  96.0 4.2 %collective-permute-done.10.refs_4_ = bf16[1024,128]{1,0:T(8,128)(2,1)S(1)} collective-permute-done((bf16[1024,128]{1,0:T(8,128)(2,1)S(1)}, bf16[1024,128]{1,0:T(8,128)(2,1)S(1)}, u32[]{:S(2)}, u32[]{:S(2)}) %collective-permute-start.10) | collective-permute-done | bytes 262176 | tf_op jit(solution)/shard_map/ppermute | solution.py:527
  100.2 1.5 collective-permute-start.15
  101.7 2.3 collective-permute-done.11.refs_5_
  105.1 24.6 %edge_stats.3 = (bf16[20,1024,128]{2,1,0:T(8,128)(2,1)}, f32[20,1024,256]{2,1,0:T(8,128)}, f32[32,2,256]{2,1,0:T(2,128)}, f32[1,256]{1,0:T(1,128)S(1)}) custom-call(s32[160,128]{1,0:T(8,128)S(1)} %reshape.101.refs_0_, bf16[1024,128]{1,0:T(8,128)(2,1)S(1)} %copy-done, bf16[1024,128]{1,0:T(8,128)(2,1)S(1)} %collective-permute-done.8.refs_2_, ...), custom_call_target="tpu_custom_call" | custom-call | bytes 66000000 | tf_op jit(solution)/shard_map/edge_stats/pallas_call | solution.py:174
  129.6 6.6 %all-to-all-start.1 = ((f32[32,2,256]{2,1,0:T(2,128)}), f32[32,2,256]{2,1,0:T(2,128)S(1)}, u32[]{:S(2)}, u32[]{:S(2)}) async-start(f32[32,2,256]{2,1,0:T(2,128)} %get-tuple-element.70), calls=%async_computation.1 | async-start | bytes 131072 | tf_op jit(solution)/shard_map/all_to_all | solution.py:504
  136.3 7.4 %all-to-all-done.1.stat_ref = f32[32,2,256]{2,1,0:T(2,128)S(1)} async-done(((f32[32,2,256]{2,1,0:T(2,128)}), f32[32,2,256]{2,1,0:T(2,128)S(1)}, u32[]{:S(2)}, u32[]{:S(2)}) %all-to-all-start.1) | async-done | bytes 65568 | tf_op jit(solution)/shard_map/all_to_all | solution.py:504
  143.7 21.4 %pool.3 = (bf16[1024,256]{1,0:T(8,128)(2,1)}, f32[20,1024,256]{2,1,0:T(8,128)}, f32[32,2,256]{2,1,0:T(2,128)}) custom-call(f32[20,1024,256]{2,1,0:T(8,128)} %get-tuple-element.69.z_ref, f32[32,2,256]{2,1,0:T(2,128)S(1)} %all-to-all-done.1.stat_ref, f32[1,256]{1,0:T(1,128)S(1)} %get-tuple-element.71.pivot_ref, f32[2,256]{1,0:T(2,128)S(1)} %pad_maximum_fusion.1.norm_ref, ...), custom_call_target="tpu_custom_call" | custom-call | bytes 60000000 | tf_op jit(solution)/shard_map/pool/pallas_call | solution.py:296
  165.1 2.6 all-to-all-start.2
  168.5 6.7 %all-to-all-done.2.grads_ref = f32[32,2,256]{2,1,0:T(2,128)S(1)} async-done(((f32[32,2,256]{2,1,0:T(2,128)}), f32[32,2,256]{2,1,0:T(2,128)S(1)}, u32[]{:S(2)}, u32[]{:S(2)}) %all-to-all-start.2) | async-done | bytes 65568 | tf_op jit(solution)/shard_map/all_to_all | solution.py:504
  175.1 37.3 %edge_grads.2 = (bf16[8192,128]{1,0:T(8,128)(2,1)}, f32[1024,256]{1,0:T(8,128)S(1)}, bf16[20,1024,256]{2,1,0:T(8,128)(2,1)}, bf16[1024,128]{1,0:T(8,128)(2,1)S(1)}) custom-call(s32[32,640]{1,0:T(8,128)S(1)} %reshape.105.idx_ref, f32[20,1024,256]{2,1,0:T(8,128)} %get-tuple-element.76.slope_ref, f32[20,1024,256]{2,1,0:T(8,128)} %get-tuple-element.69.z_ref, ...), custom_call_target="tpu_custom_call" | custom-call | bytes 105000000 | tf_op jit(solution)/shard_map/edge_grads/pallas_call | solution.py:481
  212.5 1.5 collective-permute-start.17
  214.9 2.2 collective-permute-done.16
  218.3 1.5 collective-permute-start.19
  219.8 4.9 %collective-permute-done.18 = bf16[1024,128]{1,0:T(8,128)(2,1)S(1)} collective-permute-done((bf16[1024,128]{1,0:T(8,128)(2,1)S(1)}, bf16[1024,128]{1,0:T(8,128)(2,1)S(1)}, u32[]{:S(2)}, u32[]{:S(2)}) %collective-permute-start.18) | collective-permute-done | bytes 262176 | tf_op jit(solution)/shard_map/ppermute | solution.py:559
  225.9 1.5 collective-permute-start.21
  227.4 3.8 %collective-permute-done.20 = bf16[1024,128]{1,0:T(8,128)(2,1)S(1)} collective-permute-done((bf16[1024,128]{1,0:T(8,128)(2,1)S(1)}, bf16[1024,128]{1,0:T(8,128)(2,1)S(1)}, u32[]{:S(2)}, u32[]{:S(2)}) %collective-permute-start.20) | collective-permute-done | bytes 262176 | tf_op jit(solution)/shard_map/ppermute | solution.py:559
  231.2 2.0 add_convert_fusion.6
  234.7 3.9 %collective-permute-done.22 = bf16[1024,128]{1,0:T(8,128)(2,1)S(1)} collective-permute-done((bf16[1024,128]{1,0:T(8,128)(2,1)}, bf16[1024,128]{1,0:T(8,128)(2,1)S(1)}, u32[]{:S(2)}, u32[]{:S(2)}) %collective-permute-start.22) | collective-permute-done | bytes 262176 | tf_op jit(solution)/shard_map/ppermute | solution.py:559
  239.5 1.2 convert_add_fusion.1.refs_0_
  241.6 9.4 %all-to-all-start.3 = ((f32[32,2,128]{2,1,0:T(2,128)}), f32[32,2,128]{2,1,0:T(2,128)S(1)}, u32[]{:S(2)}, u32[]{:S(2)}) async-start(f32[32,2,128]{2,1,0:T(2,128)} %broadcast_in_dim.15), calls=%async_computation.3 | async-start | bytes 65536 | tf_op jit(solution)/shard_map/all_to_all | solution.py:504
  251.0 7.8 %fusion = bf16[128,256]{1,0:T(8,128)(2,1)S(1)} fusion(bf16[20,1024,128]{2,1,0:T(8,128)(2,1)} %get-tuple-element.102, bf16[20,1024,256]{2,1,0:T(8,128)(2,1)} %get-tuple-element.103), kind=kOutput, calls=%fused_computation.2 | convolution fusion | flops 1342210048 | bytes 15794176 | tf_op jit(solution)/shard_map/kgc,kgd->cd/dot_general | solution.py:639
  259.5 34.2 %edge_grads.3 = (bf16[8192,64]{1,0:T(8,128)(2,1)}, f32[1024,128]{1,0:T(8,128)S(1)}, f32[64,128]{1,0:T(8,128)S(1)}, bf16[1024,64]{1,0:T(8,128)(2,1)S(1)}) custom-call(s32[32,640]{1,0:T(8,128)S(1)} %reshape.103.idx_ref, f32[20,1024,128]{2,1,0:T(8,128)} %get-tuple-element.74.slope_ref, f32[20,1024,128]{2,1,0:T(8,128)} %get-tuple-element.63.z_ref, ...), custom_call_target="tpu_custom_call" | custom-call | bytes 105000000 | tf_op jit(solution)/shard_map/edge_grads/pallas_call | solution.py:481
  294.1 1.4 collective-permute-start.24
  296.3 2.6 collective-permute-done.24
  301.0 1.2 collective-permute-start.26
  303.3 6.4 %all-to-all-start.4 = ((bf16[32,20,128]{2,1,0:T(8,128)(2,1)}), bf16[32,20,128]{2,1,0:T(8,128)(2,1)S(1)}, u32[]{:S(2)}, u32[]{:S(2)}) async-start(bf16[32,20,128]{2,1,0:T(8,128)(2,1)} %reshape.108), calls=%async_computation.4 | async-start | bytes 393216 | tf_op jit(solution)/shard_map/all_to_all | solution.py:504
  309.7 1.2 add_convert_fusion.2
  310.9 1.4 collective-permute-start.28
  313.0 6.7 %collective-permute-done.28 = bf16[1024,64]{1,0:T(8,128)(2,1)S(1)} collective-permute-done((bf16[1024,64]{1,0:T(8,128)(2,1)S(1)}, bf16[1024,64]{1,0:T(8,128)(2,1)S(1)}, u32[]{:S(2)}, u32[]{:S(2)}) %collective-permute-start.28) | collective-permute-done | bytes 131104 | tf_op jit(solution)/shard_map/ppermute | solution.py:559
  319.7 1.2 collective-permute-done.29
  322.1 2.1 collective-permute-start.30
  325.0 5.2 %all-to-all-start.5 = ((bf16[32,20,128]{2,1,0:T(8,128)(2,1)}), bf16[32,20,128]{2,1,0:T(8,128)(2,1)S(1)}, u32[]{:S(2)}, u32[]{:S(2)}) async-start(bf16[32,20,128]{2,1,0:T(8,128)(2,1)} %broadcast_in_dim.16), calls=%async_computation.5 | async-start | bytes 393216 | tf_op jit(solution)/shard_map/all_to_all | solution.py:504
  332.9 6.5 %all-to-all-done.5 = bf16[32,20,128]{2,1,0:T(8,128)(2,1)S(1)} async-done(((bf16[32,20,128]{2,1,0:T(8,128)(2,1)}), bf16[32,20,128]{2,1,0:T(8,128)(2,1)S(1)}, u32[]{:S(2)}, u32[]{:S(2)}) %all-to-all-start.5) | async-done | bytes 163872 | tf_op jit(solution)/shard_map/all_to_all | solution.py:504
  (135 shorter events, 29.2 us)
Async XLA Ops:
  0.6 27.3 %copy-start.4 = (bf16[128,128]{1,0:T(8,128)(2,1)S(1)}, bf16[128,128]{1,0:T(8,128)(2,1)}, u32[]{:S(2)}) copy-start(bf16[128,128]{1,0:T(8,128)(2,1)} %refs_11_.2) | copy-start | bytes 98308
  0.7 60.3 %copy-start.15 = (f32[128]{0:T(128)S(1)}, f32[128]{0:T(128)}, u32[]{:S(2)}) copy-start(f32[128]{0:T(128)} %param.16) | copy-start | bytes 1540
  0.7 60.3 %copy-start.14 = (f32[128]{0:T(128)S(1)}, f32[128]{0:T(128)}, u32[]{:S(2)}) copy-start(f32[128]{0:T(128)} %param.17) | copy-start | bytes 1540
  1.8 8.2 %collective-permute-start = (bf16[1024,64]{1,0:T(8,128)(2,1)S(1)}, bf16[1024,64]{1,0:T(8,128)(2,1)S(1)}, u32[]{:S(2)}, u32[]{:S(2)}) collective-permute-start(bf16[1024,64]{1,0:T(8,128)(2,1)S(1)} %copy.45.refs_1_.refs_10_), channel_id=1, source_target_pairs={{0,8},{8,16},{16,24},{24,28},{28,20},{20,12},{12,4},{4,0},{1,9},{9... | collective-permute-start | bytes 393224 | tf_op jit(solution)/shard_map/ppermute | solution.py:527
  3.9 7.2 %collective-permute-start.4 = (bf16[1024,64]{1,0:T(8,128)(2,1)S(1)}, bf16[1024,64]{1,0:T(8,128)(2,1)S(1)}, u32[]{:S(2)}, u32[]{:S(2)}) collective-permute-start(bf16[1024,64]{1,0:T(8,128)(2,1)S(1)} %copy.45.refs_1_.refs_10_), channel_id=1, source_target_pairs={{8,0},{16,8},{24,16},{28,24},{20,28},{12,20},{4,12},{0,4},{9,1},{1... | collective-permute-start | bytes 393224 | tf_op jit(solution)/shard_map/ppermute | solution.py:528
  9.9 6.6 %collective-permute-start.1 = (bf16[1024,64]{1,0:T(8,128)(2,1)S(1)}, bf16[1024,64]{1,0:T(8,128)(2,1)S(1)}, u32[]{:S(2)}, u32[]{:S(2)}) collective-permute-start(bf16[1024,64]{1,0:T(8,128)(2,1)S(1)} %collective-permute-done.refs_2_), channel_id=1, source_target_pairs={{0,8},{8,16},{16,24},{24,28},{28,20},{20,12},{12,4},{4,0},{1,9},{9... | collective-permute-start | bytes 393224 | tf_op jit(solution)/shard_map/ppermute | solution.py:527
  11.1 6.3 %collective-permute-start.5 = (bf16[1024,64]{1,0:T(8,128)(2,1)S(1)}, bf16[1024,64]{1,0:T(8,128)(2,1)S(1)}, u32[]{:S(2)}, u32[]{:S(2)}) collective-permute-start(bf16[1024,64]{1,0:T(8,128)(2,1)S(1)} %collective-permute-done.4.refs_9_), channel_id=1, source_target_pairs={{8,0},{16,8},{24,16},{28,24},{20,28},{12,20},{4,12},{0,4},{9,1},{1... | collective-permute-start | bytes 393224 | tf_op jit(solution)/shard_map/ppermute | solution.py:528
  16.5 5.6 %collective-permute-start.2 = (bf16[1024,64]{1,0:T(8,128)(2,1)S(1)}, bf16[1024,64]{1,0:T(8,128)(2,1)S(1)}, u32[]{:S(2)}, u32[]{:S(2)}) collective-permute-start(bf16[1024,64]{1,0:T(8,128)(2,1)S(1)} %collective-permute-done.1.refs_3_), channel_id=1, source_target_pairs={{0,8},{8,16},{16,24},{24,28},{28,20},{20,12},{12,4},{4,0},{1,9},{9... | collective-permute-start | bytes 393224 | tf_op jit(solution)/shard_map/ppermute | solution.py:527
  17.4 5.9 %collective-permute-start.6 = (bf16[1024,64]{1,0:T(8,128)(2,1)S(1)}, bf16[1024,64]{1,0:T(8,128)(2,1)S(1)}, u32[]{:S(2)}, u32[]{:S(2)}) collective-permute-start(bf16[1024,64]{1,0:T(8,128)(2,1)S(1)} %collective-permute-done.5.refs_8_), channel_id=1, source_target_pairs={{8,0},{16,8},{24,16},{28,24},{20,28},{12,20},{4,12},{0,4},{9,1},{1... | collective-permute-start | bytes 393224 | tf_op jit(solution)/shard_map/ppermute | solution.py:528
  22.8 4.6 %collective-permute-start.3 = (bf16[512,64]{1,0:T(8,128)(2,1)}, bf16[512,64]{1,0:T(8,128)(2,1)S(1)}, u32[]{:S(2)}, u32[]{:S(2)}) collective-permute-start(bf16[512,64]{1,0:T(8,128)(2,1)} %slice.138), channel_id=1, source_target_pairs={{0,8},{8,16},{16,24},{24,28},{28,20},{20,12},{12,4},{4,0},{1,9},{9... | collective-permute-start | bytes 196616 | tf_op jit(solution)/shard_map/ppermute | solution.py:530
  23.9 4.0 %collective-permute-start.7 = (bf16[512,64]{1,0:T(8,128)(2,1)}, bf16[512,64]{1,0:T(8,128)(2,1)S(1)}, u32[]{:S(2)}, u32[]{:S(2)}) collective-permute-start(bf16[512,64]{1,0:T(8,128)(2,1)} %slice.139), channel_id=1, source_target_pairs={{8,0},{16,8},{24,16},{28,24},{20,28},{12,20},{4,12},{0,4},{9,1},{1... | collective-permute-start | bytes 196616 | tf_op jit(solution)/shard_map/ppermute | solution.py:531
  51.3 16.7 %all-to-all-start = ((f32[32,2,128]{2,1,0:T(2,128)}), f32[32,2,128]{2,1,0:T(2,128)S(1)}, u32[]{:S(2)}, u32[]{:S(2)}) async-start(f32[32,2,128]{2,1,0:T(2,128)} %get-tuple-element.64), calls=%async_computation | async-start | bytes 65536 | tf_op jit(solution)/shard_map/all_to_all | solution.py:504
  68.1 36.1 %copy-start.2 = (bf16[256,256]{1,0:T(8,128)(2,1)S(1)}, bf16[256,256]{1,0:T(8,128)(2,1)}, u32[]{:S(2)}) copy-start(bf16[256,256]{1,0:T(8,128)(2,1)} %refs_11_.3) | copy-start | bytes 393220
  68.1 68.2 %copy-start.11 = (f32[256]{0:T(256)S(1)}, f32[256]{0:T(256)}, u32[]{:S(2)}) copy-start(f32[256]{0:T(256)} %param.20) | copy-start | bytes 3076
  68.1 68.2 %copy-start.12 = (f32[256]{0:T(256)S(1)}, f32[256]{0:T(256)}, u32[]{:S(2)}) copy-start(f32[256]{0:T(256)} %param.19) | copy-start | bytes 3076
  68.1 75.6 %copy-start.3 = (bf16[1024,256]{1,0:T(8,128)(2,1)S(1)}, bf16[1024,256]{1,0:T(8,128)(2,1)}, u32[]{:S(2)}) copy-start(bf16[1024,256]{1,0:T(8,128)(2,1)} %refs_0_.1) | copy-start | bytes 1572868
  80.2 7.7 %collective-permute-start.8 = (bf16[1024,128]{1,0:T(8,128)(2,1)}, bf16[1024,128]{1,0:T(8,128)(2,1)S(1)}, u32[]{:S(2)}, u32[]{:S(2)}) collective-permute-start(bf16[1024,128]{1,0:T(8,128)(2,1)} %get-tuple-element.135.refs_1_.refs_10_), channel_id=1, source_target_pairs={{0,8},{8,16},{16,24},{24,28},{28,20},{20,12},{12,4},{4,0},{1,9},{9... | collective-permute-start | bytes 786440 | tf_op jit(solution)/shard_map/ppermute | solution.py:527
  80.2 7.7 %collective-permute-start.12 = (bf16[1024,128]{1,0:T(8,128)(2,1)}, bf16[1024,128]{1,0:T(8,128)(2,1)S(1)}, u32[]{:S(2)}, u32[]{:S(2)}) collective-permute-start(bf16[1024,128]{1,0:T(8,128)(2,1)} %get-tuple-element.135.refs_1_.refs_10_), channel_id=1, source_target_pairs={{8,0},{16,8},{24,16},{28,24},{20,28},{12,20},{4,12},{0,4},{9,1},{1... | collective-permute-start | bytes 786440 | tf_op jit(solution)/shard_map/ppermute | solution.py:528
  87.9 6.6 %collective-permute-start.9 = (bf16[1024,128]{1,0:T(8,128)(2,1)S(1)}, bf16[1024,128]{1,0:T(8,128)(2,1)S(1)}, u32[]{:S(2)}, u32[]{:S(2)}) collective-permute-start(bf16[1024,128]{1,0:T(8,128)(2,1)S(1)} %collective-permute-done.8.refs_2_), channel_id=1, source_target_pairs={{0,8},{8,16},{16,24},{24,28},{28,20},{20,12},{12,4},{4,0},{1,9},{9... | collective-permute-start | bytes 786440 | tf_op jit(solution)/shard_map/ppermute | solution.py:527
  87.9 6.6 %collective-permute-start.13 = (bf16[1024,128]{1,0:T(8,128)(2,1)S(1)}, bf16[1024,128]{1,0:T(8,128)(2,1)S(1)}, u32[]{:S(2)}, u32[]{:S(2)}) collective-permute-start(bf16[1024,128]{1,0:T(8,128)(2,1)S(1)} %collective-permute-done.12.refs_9_), channel_id=1, source_target_pairs={{8,0},{16,8},{24,16},{28,24},{20,28},{12,20},{4,12},{0,4},{9,1},{1... | collective-permute-start | bytes 786440 | tf_op jit(solution)/shard_map/ppermute | solution.py:528
  94.5 5.6 %collective-permute-start.10 = (bf16[1024,128]{1,0:T(8,128)(2,1)S(1)}, bf16[1024,128]{1,0:T(8,128)(2,1)S(1)}, u32[]{:S(2)}, u32[]{:S(2)}) collective-permute-start(bf16[1024,128]{1,0:T(8,128)(2,1)S(1)} %collective-permute-done.9.refs_3_), channel_id=1, source_target_pairs={{0,8},{8,16},{16,24},{24,28},{28,20},{20,12},{12,4},{4,0},{1,9},{9... | collective-permute-start | bytes 786440 | tf_op jit(solution)/shard_map/ppermute | solution.py:527
  94.5 5.7 %collective-permute-start.14 = (bf16[1024,128]{1,0:T(8,128)(2,1)S(1)}, bf16[1024,128]{1,0:T(8,128)(2,1)S(1)}, u32[]{:S(2)}, u32[]{:S(2)}) collective-permute-start(bf16[1024,128]{1,0:T(8,128)(2,1)S(1)} %collective-permute-done.13.refs_8_), channel_id=1, source_target_pairs={{8,0},{16,8},{24,16},{28,24},{20,28},{12,20},{4,12},{0,4},{9,1},{1... | collective-permute-start | bytes 786440 | tf_op jit(solution)/shard_map/ppermute | solution.py:528
  100.1 3.9 %collective-permute-start.11 = (bf16[512,128]{1,0:T(8,128)(2,1)S(1)}, bf16[512,128]{1,0:T(8,128)(2,1)S(1)}, u32[]{:S(2)}, u32[]{:S(2)}) collective-permute-start(bf16[512,128]{1,0:T(8,128)(2,1)S(1)} %slice.140), channel_id=1, source_target_pairs={{0,8},{8,16},{16,24},{24,28},{28,20},{20,12},{12,4},{4,0},{1,9},{9... | collective-permute-start | bytes 393224 | tf_op jit(solution)/shard_map/ppermute | solution.py:530
  100.2 3.9 %collective-permute-start.15 = (bf16[512,128]{1,0:T(8,128)(2,1)S(1)}, bf16[512,128]{1,0:T(8,128)(2,1)S(1)}, u32[]{:S(2)}, u32[]{:S(2)}) collective-permute-start(bf16[512,128]{1,0:T(8,128)(2,1)S(1)} %slice.141), channel_id=1, source_target_pairs={{8,0},{16,8},{24,16},{28,24},{20,28},{12,20},{4,12},{0,4},{9,1},{1... | collective-permute-start | bytes 393224 | tf_op jit(solution)/shard_map/ppermute | solution.py:531
  129.6 14.1 %all-to-all-start.1 = ((f32[32,2,256]{2,1,0:T(2,128)}), f32[32,2,256]{2,1,0:T(2,128)S(1)}, u32[]{:S(2)}, u32[]{:S(2)}) async-start(f32[32,2,256]{2,1,0:T(2,128)} %get-tuple-element.70), calls=%async_computation.1 | async-start | bytes 131072 | tf_op jit(solution)/shard_map/all_to_all | solution.py:504
  165.1 10.0 %all-to-all-start.2 = ((f32[32,2,256]{2,1,0:T(2,128)}), f32[32,2,256]{2,1,0:T(2,128)S(1)}, u32[]{:S(2)}, u32[]{:S(2)}) async-start(f32[32,2,256]{2,1,0:T(2,128)} %get-tuple-element.77), calls=%async_computation.2 | async-start | bytes 131072 | tf_op jit(solution)/shard_map/all_to_all | solution.py:504
  175.1 38.8 %copy-start.5 = (f32[256,256]{1,0:T(8,128)S(1)}, f32[256,256]{1,0:T(8,128)}, u32[]{:S(2)}) copy-start(f32[256,256]{1,0:T(8,128)} %convert_element_type.145) | copy-start | bytes 786436
  212.4 4.7 %collective-permute-start.16 = (bf16[512,128]{1,0:T(8,128)(2,1)S(1)}, bf16[512,128]{1,0:T(8,128)(2,1)S(1)}, u32[]{:S(2)}, u32[]{:S(2)}) collective-permute-start(bf16[512,128]{1,0:T(8,128)(2,1)S(1)} %get-tuple-element.163), channel_id=1, source_target_pairs={{0,8},{8,16},{16,24},{24,28},{28,20},{20,12},{12,4},{4,0},{1,9},{9... | collective-permute-start | bytes 393224 | tf_op jit(solution)/shard_map/ppermute | solution.py:545
  212.5 4.7 %collective-permute-start.17 = (bf16[512,128]{1,0:T(8,128)(2,1)S(1)}, bf16[512,128]{1,0:T(8,128)(2,1)S(1)}, u32[]{:S(2)}, u32[]{:S(2)}) collective-permute-start(bf16[512,128]{1,0:T(8,128)(2,1)S(1)} %get-tuple-element.162), channel_id=1, source_target_pairs={{8,0},{16,8},{24,16},{28,24},{20,28},{12,20},{4,12},{0,4},{9,1},{1... | collective-permute-start | bytes 393224 | tf_op jit(solution)/shard_map/ppermute | solution.py:546
  218.3 6.4 %collective-permute-start.18 = (bf16[1024,128]{1,0:T(8,128)(2,1)S(1)}, bf16[1024,128]{1,0:T(8,128)(2,1)S(1)}, u32[]{:S(2)}, u32[]{:S(2)}) collective-permute-start(bf16[1024,128]{1,0:T(8,128)(2,1)S(1)} %get-tuple-element.84), channel_id=1, source_target_pairs={{0,8},{8,16},{16,24},{24,28},{28,20},{20,12},{12,4},{4,0},{1,9},{9... | collective-permute-start | bytes 786440 | tf_op jit(solution)/shard_map/ppermute | solution.py:559
  218.3 6.3 %collective-permute-start.19 = (bf16[1024,128]{1,0:T(8,128)(2,1)S(1)}, bf16[1024,128]{1,0:T(8,128)(2,1)S(1)}, u32[]{:S(2)}, u32[]{:S(2)}) collective-permute-start(bf16[1024,128]{1,0:T(8,128)(2,1)S(1)} %get-tuple-element.85), channel_id=1, source_target_pairs={{8,0},{16,8},{24,16},{28,24},{20,28},{12,20},{4,12},{0,4},{9,1},{1... | collective-permute-start | bytes 786440 | tf_op jit(solution)/shard_map/ppermute | solution.py:560
  225.8 5.3 %collective-permute-start.20 = (bf16[1024,128]{1,0:T(8,128)(2,1)S(1)}, bf16[1024,128]{1,0:T(8,128)(2,1)S(1)}, u32[]{:S(2)}, u32[]{:S(2)}) collective-permute-start(bf16[1024,128]{1,0:T(8,128)(2,1)S(1)} %get-tuple-element.86), channel_id=1, source_target_pairs={{0,8},{8,16},{16,24},{24,28},{28,20},{20,12},{12,4},{4,0},{1,9},{9... | collective-permute-start | bytes 786440 | tf_op jit(solution)/shard_map/ppermute | solution.py:559
  225.9 5.3 %collective-permute-start.21 = (bf16[1024,128]{1,0:T(8,128)(2,1)S(1)}, bf16[1024,128]{1,0:T(8,128)(2,1)S(1)}, u32[]{:S(2)}, u32[]{:S(2)}) collective-permute-start(bf16[1024,128]{1,0:T(8,128)(2,1)S(1)} %get-tuple-element.87), channel_id=1, source_target_pairs={{8,0},{16,8},{24,16},{28,24},{20,28},{12,20},{4,12},{0,4},{9,1},{1... | collective-permute-start | bytes 786440 | tf_op jit(solution)/shard_map/ppermute | solution.py:560
  233.1 5.4 %collective-permute-start.22 = (bf16[1024,128]{1,0:T(8,128)(2,1)}, bf16[1024,128]{1,0:T(8,128)(2,1)S(1)}, u32[]{:S(2)}, u32[]{:S(2)}) collective-permute-start(bf16[1024,128]{1,0:T(8,128)(2,1)} %get-tuple-element.88), channel_id=1, source_target_pairs={{0,8},{8,16},{16,24},{24,28},{28,20},{20,12},{12,4},{4,0},{1,9},{9... | collective-permute-start | bytes 786440 | tf_op jit(solution)/shard_map/ppermute | solution.py:559
  234.0 5.5 %collective-permute-start.23 = (bf16[1024,128]{1,0:T(8,128)(2,1)}, bf16[1024,128]{1,0:T(8,128)(2,1)}, u32[]{:S(2)}, u32[]{:S(2)}) collective-permute-start(bf16[1024,128]{1,0:T(8,128)(2,1)} %get-tuple-element.89), channel_id=1, source_target_pairs={{8,0},{16,8},{24,16},{28,24},{20,28},{12,20},{4,12},{0,4},{9,1},{1... | collective-permute-start | bytes 786440 | tf_op jit(solution)/shard_map/ppermute | solution.py:560
  241.6 17.9 %all-to-all-start.3 = ((f32[32,2,128]{2,1,0:T(2,128)}), f32[32,2,128]{2,1,0:T(2,128)S(1)}, u32[]{:S(2)}, u32[]{:S(2)}) async-start(f32[32,2,128]{2,1,0:T(2,128)} %broadcast_in_dim.15), calls=%async_computation.3 | async-start | bytes 65536 | tf_op jit(solution)/shard_map/all_to_all | solution.py:504
  259.5 34.2 %copy-start.6 = (bf16[1024,64]{0,1:T(8,128)(2,1)S(1)}, bf16[1024,64]{0,1:T(8,128)(2,1)}, u32[]{:S(2)}) copy-start(bf16[1024,64]{0,1:T(8,128)(2,1)} %param.11) | copy-start | bytes 393220
  294.1 4.9 %collective-permute-start.24 = (bf16[512,64]{1,0:T(8,128)(2,1)S(1)}, bf16[512,64]{1,0:T(8,128)(2,1)S(1)}, u32[]{:S(2)}, u32[]{:S(2)}) collective-permute-start(bf16[512,64]{1,0:T(8,128)(2,1)S(1)} %get-tuple-element.161), channel_id=1, source_target_pairs={{0,8},{8,16},{16,24},{24,28},{28,20},{20,12},{12,4},{4,0},{1,9},{9... | collective-permute-start | bytes 196616 | tf_op jit(solution)/shard_map/ppermute | solution.py:545
  295.5 4.4 %collective-permute-start.25 = (bf16[512,64]{1,0:T(8,128)(2,1)S(1)}, bf16[512,64]{1,0:T(8,128)(2,1)S(1)}, u32[]{:S(2)}, u32[]{:S(2)}) collective-permute-start(bf16[512,64]{1,0:T(8,128)(2,1)S(1)} %get-tuple-element.160), channel_id=1, source_target_pairs={{8,0},{16,8},{24,16},{28,24},{20,28},{12,20},{4,12},{0,4},{9,1},{1... | collective-permute-start | bytes 196616 | tf_op jit(solution)/shard_map/ppermute | solution.py:546
  301.0 8.7 %collective-permute-start.26 = (bf16[1024,64]{1,0:T(8,128)(2,1)S(1)}, bf16[1024,64]{1,0:T(8,128)(2,1)S(1)}, u32[]{:S(2)}, u32[]{:S(2)}) collective-permute-start(bf16[1024,64]{1,0:T(8,128)(2,1)S(1)} %get-tuple-element.107), channel_id=1, source_target_pairs={{0,8},{8,16},{16,24},{24,28},{28,20},{20,12},{12,4},{4,0},{1,9},{9... | collective-permute-start | bytes 393224 | tf_op jit(solution)/shard_map/ppermute | solution.py:559
  302.3 7.4 %collective-permute-start.27 = (bf16[1024,64]{1,0:T(8,128)(2,1)S(1)}, bf16[1024,64]{1,0:T(8,128)(2,1)S(1)}, u32[]{:S(2)}, u32[]{:S(2)}) collective-permute-start(bf16[1024,64]{1,0:T(8,128)(2,1)S(1)} %get-tuple-element.108), channel_id=1, source_target_pairs={{8,0},{16,8},{24,16},{28,24},{20,28},{12,20},{4,12},{0,4},{9,1},{1... | collective-permute-start | bytes 393224 | tf_op jit(solution)/shard_map/ppermute | solution.py:560
  302.6 38.3 %copy-start.13 = (f32[1,256]{1,0:T(1,128)}, f32[1,256]{1,0:T(1,128)S(1)}, u32[]{:S(2)}) copy-start(f32[1,256]{1,0:T(1,128)S(1)} %get-tuple-element.166) | copy-start | bytes 3076
  303.3 18.8 %all-to-all-start.4 = ((bf16[32,20,128]{2,1,0:T(8,128)(2,1)}), bf16[32,20,128]{2,1,0:T(8,128)(2,1)S(1)}, u32[]{:S(2)}, u32[]{:S(2)}) async-start(bf16[32,20,128]{2,1,0:T(8,128)(2,1)} %reshape.108), calls=%async_computation.4 | async-start | bytes 393216 | tf_op jit(solution)/shard_map/all_to_all | solution.py:504
  310.9 8.8 %collective-permute-start.28 = (bf16[1024,64]{1,0:T(8,128)(2,1)S(1)}, bf16[1024,64]{1,0:T(8,128)(2,1)S(1)}, u32[]{:S(2)}, u32[]{:S(2)}) collective-permute-start(bf16[1024,64]{1,0:T(8,128)(2,1)S(1)} %get-tuple-element.109), channel_id=1, source_target_pairs={{0,8},{8,16},{16,24},{24,28},{28,20},{20,12},{12,4},{4,0},{1,9},{9... | collective-permute-start | bytes 393224 | tf_op jit(solution)/shard_map/ppermute | solution.py:559
  312.3 8.6 %collective-permute-start.29 = (bf16[1024,64]{1,0:T(8,128)(2,1)S(1)}, bf16[1024,64]{1,0:T(8,128)(2,1)S(1)}, u32[]{:S(2)}, u32[]{:S(2)}) collective-permute-start(bf16[1024,64]{1,0:T(8,128)(2,1)S(1)} %get-tuple-element.110), channel_id=1, source_target_pairs={{8,0},{16,8},{24,16},{28,24},{20,28},{12,20},{4,12},{0,4},{9,1},{1... | collective-permute-start | bytes 393224 | tf_op jit(solution)/shard_map/ppermute | solution.py:560
  322.1 8.8 %collective-permute-start.30 = (bf16[1024,64]{1,0:T(8,128)(2,1)S(1)}, bf16[1024,64]{1,0:T(8,128)(2,1)S(1)}, u32[]{:S(2)}, u32[]{:S(2)}) collective-permute-start(bf16[1024,64]{1,0:T(8,128)(2,1)S(1)} %get-tuple-element.114), channel_id=1, source_target_pairs={{0,8},{8,16},{16,24},{24,28},{28,20},{20,12},{12,4},{4,0},{1,9},{9... | collective-permute-start | bytes 393224 | tf_op jit(solution)/shard_map/ppermute | solution.py:559
  324.2 6.7 %collective-permute-start.31 = (bf16[1024,64]{1,0:T(8,128)(2,1)S(1)}, bf16[1024,64]{1,0:T(8,128)(2,1)S(1)}, u32[]{:S(2)}, u32[]{:S(2)}) collective-permute-start(bf16[1024,64]{1,0:T(8,128)(2,1)S(1)} %get-tuple-element.115), channel_id=1, source_target_pairs={{8,0},{16,8},{24,16},{28,24},{20,28},{12,20},{4,12},{0,4},{9,1},{1... | collective-permute-start | bytes 393224 | tf_op jit(solution)/shard_map/ppermute | solution.py:560
  325.0 14.4 %all-to-all-start.5 = ((bf16[32,20,128]{2,1,0:T(8,128)(2,1)}), bf16[32,20,128]{2,1,0:T(8,128)(2,1)S(1)}, u32[]{:S(2)}, u32[]{:S(2)}) async-start(bf16[32,20,128]{2,1,0:T(8,128)(2,1)} %broadcast_in_dim.16), calls=%async_computation.5 | async-start | bytes 393216 | tf_op jit(solution)/shard_map/all_to_all | solution.py:504
  (7 other events, 74.3 us)
where the time goes:
time: 342 us; the launch traced here: 341 us
  Pallas kernels  153 us (45%)
  waiting for transfers between devices  86.4 us (25%)
  starting transfers between devices  65 us (19%)
  other arithmetic  15.2 us (4%)
  matrix products  10.4 us (3%)
  local copies, waits for them, and re-layouts  9.85 us (3%)
    pallas_call x2, Pallas kernels, edge_grads(): pl.pallas_call(functools.partial(grads_kernel, float(near * rows), bool(i...  71.5 us
    pallas_call x2, Pallas kernels, edge_stats(): pl.pallas_call(functools.partial(edge_kernel, len(pieces)), grid=(blocks...  47.9 us
    all_to_all x6, starting transfers between devices, exchange(): return lax.all_to_all(shares, BOTH, split_axis=0, concat_axis=0, tiled=True)  39.9 us
    pallas_call x2, Pallas kernels, pool(): pl.pallas_call(functools.partial(pool_kernel, cot is not None, float(near...  33.6 us
    ppermute x6, waiting for transfers between devices, line_table(): behind.append(lax.ppermute(behind[-1], 'pts', onward))  29.2 us
    all_to_all x6, waiting for transfers between devices, exchange(): return lax.all_to_all(shares, BOTH, split_axis=0, concat_axis=0, tiled=True)  27.7 us
    ppermute x6, waiting for transfers between devices, owners_sum(): forth = lax.ppermute(forth, 'pts', onward).astype(f32)  19.2 us
    dot_general x1, matrix products, per_device(): jnp.einsum('kgc,kgd->cd', diff_two, dz_two, preferred_element_type=f32)  7.77 us
  transfers between devices with their start and end apart: 38, of which 23 were waited for; matrix products, arithmetic and copies ran while one was open for 7% of the time, Pallas kernels for 0%

commit v1 on v0

--- a/solution.py
+++ b/solution.py
@@ -15,7 +15,7 @@
 GROUP = 8
 LINES = 6
 LINE_BYTES = 24 * MIB
-POINTS = 32
+TURN = 8192
 ROWS = 16
 AHEAD = 4
 LOG2E = 1.0 / math.log(2.0)
@@ -329,8 +329,9 @@
     step_id = pl.program_id(0)
     last = pl.num_programs(0) - 1
     total, rows = lines[0].shape[0], dz_sum_ref.shape[0]
-    turns = block // POINTS
-    share = near * POINTS
+    points = TURN // d
+    turns = block // points
+    share = near * points
 
     def store(waiting, most):
         while len(waiting) > most:
@@ -367,12 +368,12 @@
     rate = alpha * inv * grad_gain * (1.0 / edges)
     constant = alpha * grad_shift * (1.0 / edges) + rate * (pivot_ref[...] - mean)
     wide = [
-        [jnp.broadcast_to(x[:, lane : lane + 128], (POINTS, 128)) for x in (alpha, rate, constant)]
+        [jnp.broadcast_to(x[:, lane : lane + 128], (points, 128)) for x in (alpha, rate, constant)]
         for lane in range(0, d, 128)
     ]
 
     def turn(t, _):
-        at = pl.ds(pl.multiple_of(t * POINTS, POINTS), POINTS)
+        at = pl.ds(pl.multiple_of(t * points, points), points)
         before = jnp.maximum(step_id * turns + t - 1, 0)
         held[...] = fresh[...]
         units = [(k, i) for i in range(d // 128) for k in range(near)]
@@ -411,9 +412,9 @@
                 preferred_element_type=f32,
             )
         add(before, range(share // 2, share), waiting)
-        row = pl.multiple_of(step_id * block + t * POINTS, POINTS)
+        row = pl.multiple_of(step_id * block + t * points, points)
         for i in range(d // 128):
-            dz_sum_ref[pl.ds(row, POINTS), pl.ds(i * 128, 128)] = tree(
+            dz_sum_ref[pl.ds(row, points), pl.ds(i * 128, 128)] = tree(
                 jnp.add, [dzs[k, i].astype(f32) for k in range(near)]
             )
         store(waiting, 0)
@@ -425,7 +426,7 @@
     def _():
         held[...] = fresh[...]
         waiting = []
-        add(rows // POINTS - 1, range(share), waiting)
+        add(rows // points - 1, range(share), waiting)
         store(waiting, 0)
 
         def join(i, _):
@@ -468,8 +469,8 @@
         (dz_sum, whole(dz_sum)),
     ]
     scratch = [
-        pltpu.VMEM((near * POINTS, LANES), f32),
-        pltpu.VMEM((near * POINTS, LANES), f32),
+        pltpu.VMEM((near * (TURN // d), LANES), f32),
+        pltpu.VMEM((near * (TURN // d), LANES), f32),
         *[pltpu.VMEM((total, LANES), f32)] * turn_lines,
     ]
     if inner:
@@ -546,14 +547,13 @@
     back = lax.ppermute(send[half:], "pts", backward)
     forth, back, centre = lax.optimization_barrier((forth, back, centre))
     if weights is not None:
-        forth, back, weights = lax.optimization_barrier((forth, back, weights))
         shares = exchange(shared(weights))
     forth = jnp.pad(forth.astype(f32), ((0, half), (0, 0)))
     back = jnp.pad(back.astype(f32), ((half, 0), (0, 0)))
     for j in range(1, far):
         forth, back = (forth + slot(far + j)).astype(bf16), (back + slot(far - j)).astype(bf16)
         forth, back = lax.optimization_barrier((forth, back))
-        if weights is not None and j == far - 1:
+        if weights is not None and j == far - 2:
             forth, back, shares = lax.optimization_barrier((forth, back, shares))
             weights = everyone(jnp.sum(shares.astype(f32), axis=0).astype(bf16))
         forth = lax.ppermute(forth, "pts", onward).astype(f32)
@@ -609,8 +609,10 @@
     index_two = slot_rows(neighbours_two)
     order_one = by_blocks(index_one, BLOCK).reshape(-1, BLOCK)
     order_two = by_blocks(index_two, BLOCK).reshape(-1, BLOCK)
-    turns_one = by_blocks(index_one, POINTS).reshape(row_count // POINTS, -1)
-    turns_two = by_blocks(index_two, POINTS).reshape(row_count // POINTS, -1)
+    near = neighbours_one.shape[1]
+    points_one, points_two = TURN // gain_one.shape[0], TURN // gain_two.shape[0]
+    turns_one = by_blocks(index_one, points_one).reshape(-1, near * points_one)
+    turns_two = by_blocks(index_two, points_two).reshape(-1, near * points_two)
 
     diff_one, z_one, stat_one, pivot_one = edge_stats(order_one, table_one, points, weight_one)
     stat_one, order_two, turns_one, turns_two = lax.optimization_barrier(

time: 342 us -> 345 us (level)
  waiting for transfers between devices: 86.4 us -> 89.9 us
    all_to_all x6, waiting for transfers between devices: 27.7 us -> 21.1 us  [exchange(): return lax.all_to_all(shares, BOTH, split_axis=0, concat_axis=0, tiled=True)]
    ppermute x6, waiting for transfers between devices: 19.2 us -> 24.6 us  [owners_sum(): forth = lax.ppermute(forth, 'pts', onward).astype(f32)]
  transfers between devices with their start and end apart: 38 -> 38, of which waited for: 23 -> 25; matrix products, arithmetic and copies ran while one was open for 7% -> 7% of each run, Pallas kernels for 0% -> 0%
where the time goes in v1:
time: 345 us; the launch traced here: 343 us
  Pallas kernels  152 us (44%)
  waiting for transfers between devices  89.9 us (26%)
  starting transfers between devices  65.6 us (19%)
  other arithmetic  15.2 us (4%)
  matrix products  10.4 us (3%)
  local copies, waits for them, and re-layouts  8.98 us (3%)
    pallas_call x2, Pallas kernels, edge_grads(): pl.pallas_call(functools.partial(grads_kernel, float(near * rows), bool(i...  70.4 us
    pallas_call x2, Pallas kernels, edge_stats(): pl.pallas_call(functools.partial(edge_kernel, len(pieces)), grid=(blocks...  47.9 us
    all_to_all x6, starting transfers between devices, exchange(): return lax.all_to_all(shares, BOTH, split_axis=0, concat_axis=0, tiled=True)  40.6 us
    pallas_call x2, Pallas kernels, pool(): pl.pallas_call(functools.partial(pool_kernel, cot is not None, float(near...  33.6 us
    ppermute x6, waiting for transfers between devices, line_table(): behind.append(lax.ppermute(behind[-1], 'pts', onward))  29.2 us
    ppermute x6, waiting for transfers between devices, owners_sum(): forth = lax.ppermute(forth, 'pts', onward).astype(f32)  24.6 us
    all_to_all x6, waiting for transfers between devices, exchange(): return lax.all_to_all(shares, BOTH, split_axis=0, concat_axis=0, tiled=True)  21.1 us
    dot_general x1, matrix products, per_device(): jnp.einsum('kgc,kgd->cd', diff_two, dz_two, preferred_element_type=f32)  7.77 us
  transfers between devices with their start and end apart: 38, of which 25 were waited for; matrix products, arithmetic and copies ran while one was open for 7% of the time, Pallas kernels for 0%

profile of v1, /device:TPU:1, one launch (start us, length us, event | category | flops | bytes accessed | tf_op | source)
XLA Modules:
  0.0 343.1 jit_solution(18405414577122085536)
XLA Ops:
  1.8 2.2 collective-permute-start
  5.4 4.5 %collective-permute-done.refs_2_ = bf16[1024,64]{1,0:T(8,128)(2,1)S(1)} collective-permute-done((bf16[1024,64]{1,0:T(8,128)(2,1)S(1)}, bf16[1024,64]{1,0:T(8,128)(2,1)S(1)}, u32[]{:S(2)}, u32[]{:S(2)}) %collective-permute-start) | collective-permute-done | bytes 131104 | tf_op jit(solution)/shard_map/ppermute | solution.py:528
  9.9 1.2 collective-permute-start.1
  11.5 5.0 %collective-permute-done.1.refs_3_ = bf16[1024,64]{1,0:T(8,128)(2,1)S(1)} collective-permute-done((bf16[1024,64]{1,0:T(8,128)(2,1)S(1)}, bf16[1024,64]{1,0:T(8,128)(2,1)S(1)}, u32[]{:S(2)}, u32[]{:S(2)}) %collective-permute-start.1) | collective-permute-done | bytes 131104 | tf_op jit(solution)/shard_map/ppermute | solution.py:528
  18.0 4.2 %collective-permute-done.2.refs_4_ = bf16[1024,64]{1,0:T(8,128)(2,1)S(1)} collective-permute-done((bf16[1024,64]{1,0:T(8,128)(2,1)S(1)}, bf16[1024,64]{1,0:T(8,128)(2,1)S(1)}, u32[]{:S(2)}, u32[]{:S(2)}) %collective-permute-start.2) | collective-permute-done | bytes 131104 | tf_op jit(solution)/shard_map/ppermute | solution.py:528
  24.3 1.4 fusion.13
  27.6 23.3 %edge_stats.2 = (bf16[20,1024,64]{2,1,0:T(8,128)(2,1)}, f32[20,1024,128]{2,1,0:T(8,128)}, f32[32,2,128]{2,1,0:T(2,128)}, f32[1,128]{1,0:T(1,128)S(1)}) custom-call(s32[160,128]{1,0:T(8,128)S(1)} %reshape.99.refs_0_, bf16[1024,64]{1,0:T(8,128)(2,1)S(1)} %copy.45.refs_1_.refs_10_, bf16[1024,64]{1,0:T(8,128)(2,1)S(1)} %collective-permute-done.refs_2_, ...), custom_call_target="tpu_custom_call" | custom-call | bytes 66000000 | tf_op jit(solution)/shard_map/edge_stats/pallas_call | solution.py:174
  50.9 9.8 %all-to-all-start = ((f32[32,2,128]{2,1,0:T(2,128)}), f32[32,2,128]{2,1,0:T(2,128)S(1)}, u32[]{:S(2)}, u32[]{:S(2)}) async-start(f32[32,2,128]{2,1,0:T(2,128)} %get-tuple-element.61), calls=%async_computation | async-start | bytes 65536 | tf_op jit(solution)/shard_map/all_to_all | solution.py:505
  60.7 7.1 %all-to-all-done.stat_ref = f32[32,2,128]{2,1,0:T(2,128)S(1)} async-done(((f32[32,2,128]{2,1,0:T(2,128)}), f32[32,2,128]{2,1,0:T(2,128)S(1)}, u32[]{:S(2)}, u32[]{:S(2)}) %all-to-all-start) | async-done | bytes 32800 | tf_op jit(solution)/shard_map/all_to_all | solution.py:505
  67.8 12.1 %pool.2 = (bf16[1024,128]{1,0:T(8,128)(2,1)}, f32[20,1024,128]{2,1,0:T(8,128)}, f32[1024,128]{1,0:T(8,128)S(1)}, f32[1024,128]{1,0:T(8,128)S(1)}) custom-call(f32[20,1024,128]{2,1,0:T(8,128)} %get-tuple-element.60.z_ref, f32[32,2,128]{2,1,0:T(2,128)S(1)} %all-to-all-done.stat_ref, f32[1,128]{1,0:T(1,128)S(1)} %get-tuple-element.63.pivot_ref, ...), custom_call_target="tpu_custom_call" | custom-call | bytes 36000000 | tf_op jit(solution)/shard_map/pool/pallas_call | solution.py:296
  80.0 1.5 collective-permute-start.12
  81.4 6.2 %collective-permute-done.8.refs_2_ = bf16[1024,128]{1,0:T(8,128)(2,1)S(1)} collective-permute-done((bf16[1024,128]{1,0:T(8,128)(2,1)}, bf16[1024,128]{1,0:T(8,128)(2,1)S(1)}, u32[]{:S(2)}, u32[]{:S(2)}) %collective-permute-start.8) | collective-permute-done | bytes 262176 | tf_op jit(solution)/shard_map/ppermute | solution.py:528
  87.7 1.5 collective-permute-start.13
  89.2 5.1 %collective-permute-done.9.refs_3_ = bf16[1024,128]{1,0:T(8,128)(2,1)S(1)} collective-permute-done((bf16[1024,128]{1,0:T(8,128)(2,1)S(1)}, bf16[1024,128]{1,0:T(8,128)(2,1)S(1)}, u32[]{:S(2)}, u32[]{:S(2)}) %collective-permute-start.9) | collective-permute-done | bytes 262176 | tf_op jit(solution)/shard_map/ppermute | solution.py:528
  94.3 1.5 collective-permute-start.14
  95.7 4.2 %collective-permute-done.10.refs_4_ = bf16[1024,128]{1,0:T(8,128)(2,1)S(1)} collective-permute-done((bf16[1024,128]{1,0:T(8,128)(2,1)S(1)}, bf16[1024,128]{1,0:T(8,128)(2,1)S(1)}, u32[]{:S(2)}, u32[]{:S(2)}) %collective-permute-start.10) | collective-permute-done | bytes 262176 | tf_op jit(solution)/shard_map/ppermute | solution.py:528
  100.0 1.5 collective-permute-start.15
  101.5 2.3 collective-permute-done.11.refs_5_
  104.8 24.6 %edge_stats.3 = (bf16[20,1024,128]{2,1,0:T(8,128)(2,1)}, f32[20,1024,256]{2,1,0:T(8,128)}, f32[32,2,256]{2,1,0:T(2,128)}, f32[1,256]{1,0:T(1,128)S(1)}) custom-call(s32[160,128]{1,0:T(8,128)S(1)} %reshape.101.refs_0_, bf16[1024,128]{1,0:T(8,128)(2,1)S(1)} %copy-done, bf16[1024,128]{1,0:T(8,128)(2,1)S(1)} %collective-permute-done.8.refs_2_, ...), custom_call_target="tpu_custom_call" | custom-call | bytes 66000000 | tf_op jit(solution)/shard_map/edge_stats/pallas_call | solution.py:174
  129.4 6.7 %all-to-all-start.1 = ((f32[32,2,256]{2,1,0:T(2,128)}), f32[32,2,256]{2,1,0:T(2,128)S(1)}, u32[]{:S(2)}, u32[]{:S(2)}) async-start(f32[32,2,256]{2,1,0:T(2,128)} %get-tuple-element.67), calls=%async_computation.1 | async-start | bytes 131072 | tf_op jit(solution)/shard_map/all_to_all | solution.py:505
  136.1 7.4 %all-to-all-done.1.stat_ref = f32[32,2,256]{2,1,0:T(2,128)S(1)} async-done(((f32[32,2,256]{2,1,0:T(2,128)}), f32[32,2,256]{2,1,0:T(2,128)S(1)}, u32[]{:S(2)}, u32[]{:S(2)}) %all-to-all-start.1) | async-done | bytes 65568 | tf_op jit(solution)/shard_map/all_to_all | solution.py:505
  143.5 21.4 %pool.3 = (bf16[1024,256]{1,0:T(8,128)(2,1)}, f32[20,1024,256]{2,1,0:T(8,128)}, f32[32,2,256]{2,1,0:T(2,128)}) custom-call(f32[20,1024,256]{2,1,0:T(8,128)} %get-tuple-element.66.z_ref, f32[32,2,256]{2,1,0:T(2,128)S(1)} %all-to-all-done.1.stat_ref, f32[1,256]{1,0:T(1,128)S(1)} %get-tuple-element.68.pivot_ref, f32[2,256]{1,0:T(2,128)S(1)} %pad_maximum_fusion.1.norm_ref, ...), custom_call_target="tpu_custom_call" | custom-call | bytes 60000000 | tf_op jit(solution)/shard_map/pool/pallas_call | solution.py:296
  164.9 2.6 all-to-all-start.2
  168.3 6.7 %all-to-all-done.2.grads_ref = f32[32,2,256]{2,1,0:T(2,128)S(1)} async-done(((f32[32,2,256]{2,1,0:T(2,128)}), f32[32,2,256]{2,1,0:T(2,128)S(1)}, u32[]{:S(2)}, u32[]{:S(2)}) %all-to-all-start.2) | async-done | bytes 65568 | tf_op jit(solution)/shard_map/all_to_all | solution.py:505
  174.9 37.3 %edge_grads.2 = (bf16[8192,128]{1,0:T(8,128)(2,1)}, f32[1024,256]{1,0:T(8,128)S(1)}, bf16[20,1024,256]{2,1,0:T(8,128)(2,1)}, bf16[1024,128]{1,0:T(8,128)(2,1)S(1)}) custom-call(s32[32,640]{1,0:T(8,128)S(1)} %reshape.105.idx_ref, f32[20,1024,256]{2,1,0:T(8,128)} %get-tuple-element.73.slope_ref, f32[20,1024,256]{2,1,0:T(8,128)} %get-tuple-element.66.z_ref, ...), custom_call_target="tpu_custom_call" | custom-call | bytes 105000000 | tf_op jit(solution)/shard_map/edge_grads/pallas_call | solution.py:482
  212.3 1.5 collective-permute-start.17
  214.7 2.2 collective-permute-done.16
  218.1 1.5 collective-permute-start.19
  219.6 4.9 %collective-permute-done.18 = bf16[1024,128]{1,0:T(8,128)(2,1)S(1)} collective-permute-done((bf16[1024,128]{1,0:T(8,128)(2,1)S(1)}, bf16[1024,128]{1,0:T(8,128)(2,1)S(1)}, u32[]{:S(2)}, u32[]{:S(2)}) %collective-permute-start.18) | collective-permute-done | bytes 262176 | tf_op jit(solution)/shard_map/ppermute | solution.py:559
  225.7 1.5 collective-permute-start.21
  227.2 3.8 %collective-permute-done.20 = bf16[1024,128]{1,0:T(8,128)(2,1)S(1)} collective-permute-done((bf16[1024,128]{1,0:T(8,128)(2,1)S(1)}, bf16[1024,128]{1,0:T(8,128)(2,1)S(1)}, u32[]{:S(2)}, u32[]{:S(2)}) %collective-permute-start.20) | collective-permute-done | bytes 262176 | tf_op jit(solution)/shard_map/ppermute | solution.py:559
  231.0 2.0 add_convert_fusion.6
  234.5 3.9 %collective-permute-done.22 = bf16[1024,128]{1,0:T(8,128)(2,1)S(1)} collective-permute-done((bf16[1024,128]{1,0:T(8,128)(2,1)}, bf16[1024,128]{1,0:T(8,128)(2,1)S(1)}, u32[]{:S(2)}, u32[]{:S(2)}) %collective-permute-start.22) | collective-permute-done | bytes 262176 | tf_op jit(solution)/shard_map/ppermute | solution.py:559
  239.3 1.2 convert_add_fusion.1.refs_0_
  241.4 9.4 %all-to-all-start.3 = ((f32[32,2,128]{2,1,0:T(2,128)}), f32[32,2,128]{2,1,0:T(2,128)S(1)}, u32[]{:S(2)}, u32[]{:S(2)}) async-start(f32[32,2,128]{2,1,0:T(2,128)} %broadcast_in_dim.15), calls=%async_computation.3 | async-start | bytes 65536 | tf_op jit(solution)/shard_map/all_to_all | solution.py:505
  250.8 7.8 %fusion = bf16[128,256]{1,0:T(8,128)(2,1)S(1)} fusion(bf16[20,1024,128]{2,1,0:T(8,128)(2,1)} %get-tuple-element.103, bf16[20,1024,256]{2,1,0:T(8,128)(2,1)} %get-tuple-element.104), kind=kOutput, calls=%fused_computation.2 | convolution fusion | flops 1342210048 | bytes 15794176 | tf_op jit(solution)/shard_map/kgc,kgd->cd/dot_general | solution.py:641
  259.3 33.1 %edge_grads.3 = (bf16[8192,64]{1,0:T(8,128)(2,1)}, f32[1024,128]{1,0:T(8,128)S(1)}, f32[64,128]{1,0:T(8,128)S(1)}, bf16[1024,64]{1,0:T(8,128)(2,1)S(1)}) custom-call(s32[16,1280]{1,0:T(8,128)S(1)} %reshape.103.idx_ref, f32[20,1024,128]{2,1,0:T(8,128)} %get-tuple-element.71.slope_ref, f32[20,1024,128]{2,1,0:T(8,128)} %get-tuple-element.60.z_ref, ...), custom_call_target="tpu_custom_call" | custom-call | bytes 105000000 | tf_op jit(solution)/shard_map/edge_grads/pallas_call | solution.py:482
  293.5 5.8 %all-to-all-start.4 = ((bf16[32,20,128]{2,1,0:T(8,128)(2,1)}), bf16[32,20,128]{2,1,0:T(8,128)(2,1)S(1)}, u32[]{:S(2)}, u32[]{:S(2)}) async-start(bf16[32,20,128]{2,1,0:T(8,128)(2,1)} %convert_element_type.181), calls=%async_computation.4 | async-start | bytes 393216 | tf_op jit(solution)/shard_map/all_to_all | solution.py:505
  299.3 1.4 collective-permute-start.24
  301.6 4.3 %collective-permute-done.24 = bf16[512,64]{1,0:T(8,128)(2,1)S(1)} collective-permute-done((bf16[512,64]{1,0:T(8,128)(2,1)S(1)}, bf16[512,64]{1,0:T(8,128)(2,1)S(1)}, u32[]{:S(2)}, u32[]{:S(2)}) %collective-permute-start.24) | collective-permute-done | bytes 65568 | tf_op jit(solution)/shard_map/ppermute | solution.py:546
  305.8 1.8 collective-permute-done.25
  308.8 2.2 collective-permute-start.26
  311.0 4.8 %collective-permute-done.26 = bf16[1024,64]{1,0:T(8,128)(2,1)S(1)} collective-permute-done((bf16[1024,64]{1,0:T(8,128)(2,1)S(1)}, bf16[1024,64]{1,0:T(8,128)(2,1)S(1)}, u32[]{:S(2)}, u32[]{:S(2)}) %collective-permute-start.26) | collective-permute-done | bytes 131104 | tf_op jit(solution)/shard_map/ppermute | solution.py:559
  315.7 1.9 collective-permute-done.27
  321.7 6.3 %all-to-all-start.5 = ((bf16[32,20,128]{2,1,0:T(8,128)(2,1)}), bf16[32,20,128]{2,1,0:T(8,128)(2,1)S(1)}, u32[]{:S(2)}, u32[]{:S(2)}) async-start(bf16[32,20,128]{2,1,0:T(8,128)(2,1)} %broadcast_in_dim.16), calls=%async_computation.5 | async-start | bytes 393216 | tf_op jit(solution)/shard_map/all_to_all | solution.py:505
  328.0 1.2 add_convert_fusion
  329.2 1.4 collective-permute-start.30
  331.4 7.3 %collective-permute-done.30 = bf16[1024,64]{1,0:T(8,128)(2,1)S(1)} collective-permute-done((bf16[1024,64]{1,0:T(8,128)(2,1)S(1)}, bf16[1024,64]{1,0:T(8,128)(2,1)S(1)}, u32[]{:S(2)}, u32[]{:S(2)}) %collective-permute-start.30) | collective-permute-done | bytes 131104 | tf_op jit(solution)/shard_map/ppermute | solution.py:559
  (135 shorter events, 30.0 us)
Async XLA Ops:
  0.6 27.0 %copy-start.4 = (bf16[128,128]{1,0:T(8,128)(2,1)S(1)}, bf16[128,128]{1,0:T(8,128)(2,1)}, u32[]{:S(2)}) copy-start(bf16[128,128]{1,0:T(8,128)(2,1)} %refs_11_.2) | copy-start | bytes 98308
  0.7 60.1 %copy-start.15 = (f32[128]{0:T(128)S(1)}, f32[128]{0:T(128)}, u32[]{:S(2)}) copy-start(f32[128]{0:T(128)} %param.16) | copy-start | bytes 1540
  0.7 60.1 %copy-start.14 = (f32[128]{0:T(128)S(1)}, f32[128]{0:T(128)}, u32[]{:S(2)}) copy-start(f32[128]{0:T(128)} %param.17) | copy-start | bytes 1540
  1.8 8.2 %collective-permute-start = (bf16[1024,64]{1,0:T(8,128)(2,1)S(1)}, bf16[1024,64]{1,0:T(8,128)(2,1)S(1)}, u32[]{:S(2)}, u32[]{:S(2)}) collective-permute-start(bf16[1024,64]{1,0:T(8,128)(2,1)S(1)} %copy.45.refs_1_.refs_10_), channel_id=1, source_target_pairs={{0,8},{8,16},{16,24},{24,28},{28,20},{20,12},{12,4},{4,0},{1,9},{9... | collective-permute-start | bytes 393224 | tf_op jit(solution)/shard_map/ppermute | solution.py:528
  3.9 7.2 %collective-permute-start.4 = (bf16[1024,64]{1,0:T(8,128)(2,1)S(1)}, bf16[1024,64]{1,0:T(8,128)(2,1)S(1)}, u32[]{:S(2)}, u32[]{:S(2)}) collective-permute-start(bf16[1024,64]{1,0:T(8,128)(2,1)S(1)} %copy.45.refs_1_.refs_10_), channel_id=1, source_target_pairs={{8,0},{16,8},{24,16},{28,24},{20,28},{12,20},{4,12},{0,4},{9,1},{1... | collective-permute-start | bytes 393224 | tf_op jit(solution)/shard_map/ppermute | solution.py:529
  9.9 6.6 %collective-permute-start.1 = (bf16[1024,64]{1,0:T(8,128)(2,1)S(1)}, bf16[1024,64]{1,0:T(8,128)(2,1)S(1)}, u32[]{:S(2)}, u32[]{:S(2)}) collective-permute-start(bf16[1024,64]{1,0:T(8,128)(2,1)S(1)} %collective-permute-done.refs_2_), channel_id=1, source_target_pairs={{0,8},{8,16},{16,24},{24,28},{28,20},{20,12},{12,4},{4,0},{1,9},{9... | collective-permute-start | bytes 393224 | tf_op jit(solution)/shard_map/ppermute | solution.py:528
  11.1 6.3 %collective-permute-start.5 = (bf16[1024,64]{1,0:T(8,128)(2,1)S(1)}, bf16[1024,64]{1,0:T(8,128)(2,1)S(1)}, u32[]{:S(2)}, u32[]{:S(2)}) collective-permute-start(bf16[1024,64]{1,0:T(8,128)(2,1)S(1)} %collective-permute-done.4.refs_9_), channel_id=1, source_target_pairs={{8,0},{16,8},{24,16},{28,24},{20,28},{12,20},{4,12},{0,4},{9,1},{1... | collective-permute-start | bytes 393224 | tf_op jit(solution)/shard_map/ppermute | solution.py:529
  16.5 5.6 %collective-permute-start.2 = (bf16[1024,64]{1,0:T(8,128)(2,1)S(1)}, bf16[1024,64]{1,0:T(8,128)(2,1)S(1)}, u32[]{:S(2)}, u32[]{:S(2)}) collective-permute-start(bf16[1024,64]{1,0:T(8,128)(2,1)S(1)} %collective-permute-done.1.refs_3_), channel_id=1, source_target_pairs={{0,8},{8,16},{16,24},{24,28},{28,20},{20,12},{12,4},{4,0},{1,9},{9... | collective-permute-start | bytes 393224 | tf_op jit(solution)/shard_map/ppermute | solution.py:528
  17.4 5.5 %collective-permute-start.6 = (bf16[1024,64]{1,0:T(8,128)(2,1)S(1)}, bf16[1024,64]{1,0:T(8,128)(2,1)S(1)}, u32[]{:S(2)}, u32[]{:S(2)}) collective-permute-start(bf16[1024,64]{1,0:T(8,128)(2,1)S(1)} %collective-permute-done.5.refs_8_), channel_id=1, source_target_pairs={{8,0},{16,8},{24,16},{28,24},{20,28},{12,20},{4,12},{0,4},{9,1},{1... | collective-permute-start | bytes 393224 | tf_op jit(solution)/shard_map/ppermute | solution.py:529
  22.2 4.5 %collective-permute-start.3 = (bf16[512,64]{1,0:T(8,128)(2,1)S(1)}, bf16[512,64]{1,0:T(8,128)(2,1)S(1)}, u32[]{:S(2)}, u32[]{:S(2)}) collective-permute-start(bf16[512,64]{1,0:T(8,128)(2,1)S(1)} %slice.138), channel_id=1, source_target_pairs={{0,8},{8,16},{16,24},{24,28},{28,20},{20,12},{12,4},{4,0},{1,9},{9... | collective-permute-start | bytes 196616 | tf_op jit(solution)/shard_map/ppermute | solution.py:531
  23.6 4.0 %collective-permute-start.7 = (bf16[512,64]{1,0:T(8,128)(2,1)}, bf16[512,64]{1,0:T(8,128)(2,1)S(1)}, u32[]{:S(2)}, u32[]{:S(2)}) collective-permute-start(bf16[512,64]{1,0:T(8,128)(2,1)} %slice.139), channel_id=1, source_target_pairs={{8,0},{16,8},{24,16},{28,24},{20,28},{12,20},{4,12},{0,4},{9,1},{1... | collective-permute-start | bytes 196616 | tf_op jit(solution)/shard_map/ppermute | solution.py:532
  50.9 16.9 %all-to-all-start = ((f32[32,2,128]{2,1,0:T(2,128)}), f32[32,2,128]{2,1,0:T(2,128)S(1)}, u32[]{:S(2)}, u32[]{:S(2)}) async-start(f32[32,2,128]{2,1,0:T(2,128)} %get-tuple-element.61), calls=%async_computation | async-start | bytes 65536 | tf_op jit(solution)/shard_map/all_to_all | solution.py:505
  67.8 36.1 %copy-start.2 = (bf16[256,256]{1,0:T(8,128)(2,1)S(1)}, bf16[256,256]{1,0:T(8,128)(2,1)}, u32[]{:S(2)}) copy-start(bf16[256,256]{1,0:T(8,128)(2,1)} %refs_11_.3) | copy-start | bytes 393220
  67.8 68.3 %copy-start.11 = (f32[256]{0:T(256)S(1)}, f32[256]{0:T(256)}, u32[]{:S(2)}) copy-start(f32[256]{0:T(256)} %param.20) | copy-start | bytes 3076
  67.8 68.3 %copy-start.12 = (f32[256]{0:T(256)S(1)}, f32[256]{0:T(256)}, u32[]{:S(2)}) copy-start(f32[256]{0:T(256)} %param.19) | copy-start | bytes 3076
  67.8 75.7 %copy-start.3 = (bf16[1024,256]{1,0:T(8,128)(2,1)S(1)}, bf16[1024,256]{1,0:T(8,128)(2,1)}, u32[]{:S(2)}) copy-start(bf16[1024,256]{1,0:T(8,128)(2,1)} %refs_0_.1) | copy-start | bytes 1572868
  80.0 7.7 %collective-permute-start.8 = (bf16[1024,128]{1,0:T(8,128)(2,1)}, bf16[1024,128]{1,0:T(8,128)(2,1)S(1)}, u32[]{:S(2)}, u32[]{:S(2)}) collective-permute-start(bf16[1024,128]{1,0:T(8,128)(2,1)} %get-tuple-element.129.refs_1_.refs_10_), channel_id=1, source_target_pairs={{0,8},{8,16},{16,24},{24,28},{28,20},{20,12},{12,4},{4,0},{1,9},{9... | collective-permute-start | bytes 786440 | tf_op jit(solution)/shard_map/ppermute | solution.py:528
  80.0 7.7 %collective-permute-start.12 = (bf16[1024,128]{1,0:T(8,128)(2,1)}, bf16[1024,128]{1,0:T(8,128)(2,1)S(1)}, u32[]{:S(2)}, u32[]{:S(2)}) collective-permute-start(bf16[1024,128]{1,0:T(8,128)(2,1)} %get-tuple-element.129.refs_1_.refs_10_), channel_id=1, source_target_pairs={{8,0},{16,8},{24,16},{28,24},{20,28},{12,20},{4,12},{0,4},{9,1},{1... | collective-permute-start | bytes 786440 | tf_op jit(solution)/shard_map/ppermute | solution.py:529
  87.7 6.6 %collective-permute-start.9 = (bf16[1024,128]{1,0:T(8,128)(2,1)S(1)}, bf16[1024,128]{1,0:T(8,128)(2,1)S(1)}, u32[]{:S(2)}, u32[]{:S(2)}) collective-permute-start(bf16[1024,128]{1,0:T(8,128)(2,1)S(1)} %collective-permute-done.8.refs_2_), channel_id=1, source_target_pairs={{0,8},{8,16},{16,24},{24,28},{28,20},{20,12},{12,4},{4,0},{1,9},{9... | collective-permute-start | bytes 786440 | tf_op jit(solution)/shard_map/ppermute | solution.py:528
  87.7 6.6 %collective-permute-start.13 = (bf16[1024,128]{1,0:T(8,128)(2,1)S(1)}, bf16[1024,128]{1,0:T(8,128)(2,1)S(1)}, u32[]{:S(2)}, u32[]{:S(2)}) collective-permute-start(bf16[1024,128]{1,0:T(8,128)(2,1)S(1)} %collective-permute-done.12.refs_9_), channel_id=1, source_target_pairs={{8,0},{16,8},{24,16},{28,24},{20,28},{12,20},{4,12},{0,4},{9,1},{1... | collective-permute-start | bytes 786440 | tf_op jit(solution)/shard_map/ppermute | solution.py:529
  94.3 5.6 %collective-permute-start.10 = (bf16[1024,128]{1,0:T(8,128)(2,1)S(1)}, bf16[1024,128]{1,0:T(8,128)(2,1)S(1)}, u32[]{:S(2)}, u32[]{:S(2)}) collective-permute-start(bf16[1024,128]{1,0:T(8,128)(2,1)S(1)} %collective-permute-done.9.refs_3_), channel_id=1, source_target_pairs={{0,8},{8,16},{16,24},{24,28},{28,20},{20,12},{12,4},{4,0},{1,9},{9... | collective-permute-start | bytes 786440 | tf_op jit(solution)/shard_map/ppermute | solution.py:528
  94.3 5.7 %collective-permute-start.14 = (bf16[1024,128]{1,0:T(8,128)(2,1)S(1)}, bf16[1024,128]{1,0:T(8,128)(2,1)S(1)}, u32[]{:S(2)}, u32[]{:S(2)}) collective-permute-start(bf16[1024,128]{1,0:T(8,128)(2,1)S(1)} %collective-permute-done.13.refs_8_), channel_id=1, source_target_pairs={{8,0},{16,8},{24,16},{28,24},{20,28},{12,20},{4,12},{0,4},{9,1},{1... | collective-permute-start | bytes 786440 | tf_op jit(solution)/shard_map/ppermute | solution.py:529
  99.9 3.9 %collective-permute-start.11 = (bf16[512,128]{1,0:T(8,128)(2,1)S(1)}, bf16[512,128]{1,0:T(8,128)(2,1)S(1)}, u32[]{:S(2)}, u32[]{:S(2)}) collective-permute-start(bf16[512,128]{1,0:T(8,128)(2,1)S(1)} %slice.140), channel_id=1, source_target_pairs={{0,8},{8,16},{16,24},{24,28},{28,20},{20,12},{12,4},{4,0},{1,9},{9... | collective-permute-start | bytes 393224 | tf_op jit(solution)/shard_map/ppermute | solution.py:531
  100.0 3.9 %collective-permute-start.15 = (bf16[512,128]{1,0:T(8,128)(2,1)S(1)}, bf16[512,128]{1,0:T(8,128)(2,1)S(1)}, u32[]{:S(2)}, u32[]{:S(2)}) collective-permute-start(bf16[512,128]{1,0:T(8,128)(2,1)S(1)} %slice.141), channel_id=1, source_target_pairs={{8,0},{16,8},{24,16},{28,24},{20,28},{12,20},{4,12},{0,4},{9,1},{1... | collective-permute-start | bytes 393224 | tf_op jit(solution)/shard_map/ppermute | solution.py:532
  129.4 14.1 %all-to-all-start.1 = ((f32[32,2,256]{2,1,0:T(2,128)}), f32[32,2,256]{2,1,0:T(2,128)S(1)}, u32[]{:S(2)}, u32[]{:S(2)}) async-start(f32[32,2,256]{2,1,0:T(2,128)} %get-tuple-element.67), calls=%async_computation.1 | async-start | bytes 131072 | tf_op jit(solution)/shard_map/all_to_all | solution.py:505
  164.9 10.0 %all-to-all-start.2 = ((f32[32,2,256]{2,1,0:T(2,128)}), f32[32,2,256]{2,1,0:T(2,128)S(1)}, u32[]{:S(2)}, u32[]{:S(2)}) async-start(f32[32,2,256]{2,1,0:T(2,128)} %get-tuple-element.74), calls=%async_computation.2 | async-start | bytes 131072 | tf_op jit(solution)/shard_map/all_to_all | solution.py:505
  174.9 38.8 %copy-start.5 = (f32[256,256]{1,0:T(8,128)S(1)}, f32[256,256]{1,0:T(8,128)}, u32[]{:S(2)}) copy-start(f32[256,256]{1,0:T(8,128)} %convert_element_type.149) | copy-start | bytes 786436
  212.2 4.7 %collective-permute-start.16 = (bf16[512,128]{1,0:T(8,128)(2,1)S(1)}, bf16[512,128]{1,0:T(8,128)(2,1)S(1)}, u32[]{:S(2)}, u32[]{:S(2)}) collective-permute-start(bf16[512,128]{1,0:T(8,128)(2,1)S(1)} %get-tuple-element.157), channel_id=1, source_target_pairs={{0,8},{8,16},{16,24},{24,28},{28,20},{20,12},{12,4},{4,0},{1,9},{9... | collective-permute-start | bytes 393224 | tf_op jit(solution)/shard_map/ppermute | solution.py:546
  212.3 4.7 %collective-permute-start.17 = (bf16[512,128]{1,0:T(8,128)(2,1)S(1)}, bf16[512,128]{1,0:T(8,128)(2,1)S(1)}, u32[]{:S(2)}, u32[]{:S(2)}) collective-permute-start(bf16[512,128]{1,0:T(8,128)(2,1)S(1)} %get-tuple-element.156), channel_id=1, source_target_pairs={{8,0},{16,8},{24,16},{28,24},{20,28},{12,20},{4,12},{0,4},{9,1},{1... | collective-permute-start | bytes 393224 | tf_op jit(solution)/shard_map/ppermute | solution.py:547
  218.1 6.4 %collective-permute-start.18 = (bf16[1024,128]{1,0:T(8,128)(2,1)S(1)}, bf16[1024,128]{1,0:T(8,128)(2,1)S(1)}, u32[]{:S(2)}, u32[]{:S(2)}) collective-permute-start(bf16[1024,128]{1,0:T(8,128)(2,1)S(1)} %get-tuple-element.81), channel_id=1, source_target_pairs={{0,8},{8,16},{16,24},{24,28},{28,20},{20,12},{12,4},{4,0},{1,9},{9... | collective-permute-start | bytes 786440 | tf_op jit(solution)/shard_map/ppermute | solution.py:559
  218.1 6.3 %collective-permute-start.19 = (bf16[1024,128]{1,0:T(8,128)(2,1)S(1)}, bf16[1024,128]{1,0:T(8,128)(2,1)S(1)}, u32[]{:S(2)}, u32[]{:S(2)}) collective-permute-start(bf16[1024,128]{1,0:T(8,128)(2,1)S(1)} %get-tuple-element.82), channel_id=1, source_target_pairs={{8,0},{16,8},{24,16},{28,24},{20,28},{12,20},{4,12},{0,4},{9,1},{1... | collective-permute-start | bytes 786440 | tf_op jit(solution)/shard_map/ppermute | solution.py:560
  225.6 5.3 %collective-permute-start.20 = (bf16[1024,128]{1,0:T(8,128)(2,1)S(1)}, bf16[1024,128]{1,0:T(8,128)(2,1)S(1)}, u32[]{:S(2)}, u32[]{:S(2)}) collective-permute-start(bf16[1024,128]{1,0:T(8,128)(2,1)S(1)} %get-tuple-element.83), channel_id=1, source_target_pairs={{0,8},{8,16},{16,24},{24,28},{28,20},{20,12},{12,4},{4,0},{1,9},{9... | collective-permute-start | bytes 786440 | tf_op jit(solution)/shard_map/ppermute | solution.py:559
  225.7 5.3 %collective-permute-start.21 = (bf16[1024,128]{1,0:T(8,128)(2,1)S(1)}, bf16[1024,128]{1,0:T(8,128)(2,1)S(1)}, u32[]{:S(2)}, u32[]{:S(2)}) collective-permute-start(bf16[1024,128]{1,0:T(8,128)(2,1)S(1)} %get-tuple-element.84), channel_id=1, source_target_pairs={{8,0},{16,8},{24,16},{28,24},{20,28},{12,20},{4,12},{0,4},{9,1},{1... | collective-permute-start | bytes 786440 | tf_op jit(solution)/shard_map/ppermute | solution.py:560
  232.9 5.4 %collective-permute-start.22 = (bf16[1024,128]{1,0:T(8,128)(2,1)}, bf16[1024,128]{1,0:T(8,128)(2,1)S(1)}, u32[]{:S(2)}, u32[]{:S(2)}) collective-permute-start(bf16[1024,128]{1,0:T(8,128)(2,1)} %get-tuple-element.85), channel_id=1, source_target_pairs={{0,8},{8,16},{16,24},{24,28},{28,20},{20,12},{12,4},{4,0},{1,9},{9... | collective-permute-start | bytes 786440 | tf_op jit(solution)/shard_map/ppermute | solution.py:559
  233.8 5.5 %collective-permute-start.23 = (bf16[1024,128]{1,0:T(8,128)(2,1)}, bf16[1024,128]{1,0:T(8,128)(2,1)}, u32[]{:S(2)}, u32[]{:S(2)}) collective-permute-start(bf16[1024,128]{1,0:T(8,128)(2,1)} %get-tuple-element.86), channel_id=1, source_target_pairs={{8,0},{16,8},{24,16},{28,24},{20,28},{12,20},{4,12},{0,4},{9,1},{1... | collective-permute-start | bytes 786440 | tf_op jit(solution)/shard_map/ppermute | solution.py:560
  241.4 17.9 %all-to-all-start.3 = ((f32[32,2,128]{2,1,0:T(2,128)}), f32[32,2,128]{2,1,0:T(2,128)S(1)}, u32[]{:S(2)}, u32[]{:S(2)}) async-start(f32[32,2,128]{2,1,0:T(2,128)} %broadcast_in_dim.15), calls=%async_computation.3 | async-start | bytes 65536 | tf_op jit(solution)/shard_map/all_to_all | solution.py:505
  259.3 33.1 %copy-start.6 = (bf16[1024,64]{0,1:T(8,128)(2,1)S(1)}, bf16[1024,64]{0,1:T(8,128)(2,1)}, u32[]{:S(2)}) copy-start(bf16[1024,64]{0,1:T(8,128)(2,1)} %param.11) | copy-start | bytes 393220
  293.5 25.3 %all-to-all-start.4 = ((bf16[32,20,128]{2,1,0:T(8,128)(2,1)}), bf16[32,20,128]{2,1,0:T(8,128)(2,1)S(1)}, u32[]{:S(2)}, u32[]{:S(2)}) async-start(bf16[32,20,128]{2,1,0:T(8,128)(2,1)} %convert_element_type.181), calls=%async_computation.4 | async-start | bytes 393216 | tf_op jit(solution)/shard_map/all_to_all | solution.py:505
  299.3 6.5 %collective-permute-start.24 = (bf16[512,64]{1,0:T(8,128)(2,1)S(1)}, bf16[512,64]{1,0:T(8,128)(2,1)S(1)}, u32[]{:S(2)}, u32[]{:S(2)}) collective-permute-start(bf16[512,64]{1,0:T(8,128)(2,1)S(1)} %get-tuple-element.155), channel_id=1, source_target_pairs={{0,8},{8,16},{16,24},{24,28},{28,20},{20,12},{12,4},{4,0},{1,9},{9... | collective-permute-start | bytes 196616 | tf_op jit(solution)/shard_map/ppermute | solution.py:546
  300.8 6.9 %collective-permute-start.25 = (bf16[512,64]{1,0:T(8,128)(2,1)S(1)}, bf16[512,64]{1,0:T(8,128)(2,1)S(1)}, u32[]{:S(2)}, u32[]{:S(2)}) collective-permute-start(bf16[512,64]{1,0:T(8,128)(2,1)S(1)} %get-tuple-element.154), channel_id=1, source_target_pairs={{8,0},{16,8},{24,16},{28,24},{20,28},{12,20},{4,12},{0,4},{9,1},{1... | collective-permute-start | bytes 196616 | tf_op jit(solution)/shard_map/ppermute | solution.py:547
  308.8 6.9 %collective-permute-start.26 = (bf16[1024,64]{1,0:T(8,128)(2,1)S(1)}, bf16[1024,64]{1,0:T(8,128)(2,1)S(1)}, u32[]{:S(2)}, u32[]{:S(2)}) collective-permute-start(bf16[1024,64]{1,0:T(8,128)(2,1)S(1)} %get-tuple-element.98), channel_id=1, source_target_pairs={{0,8},{8,16},{16,24},{24,28},{28,20},{20,12},{12,4},{4,0},{1,9},{9... | collective-permute-start | bytes 393224 | tf_op jit(solution)/shard_map/ppermute | solution.py:559
  311.0 6.6 %collective-permute-start.27 = (bf16[1024,64]{1,0:T(8,128)(2,1)S(1)}, bf16[1024,64]{1,0:T(8,128)(2,1)S(1)}, u32[]{:S(2)}, u32[]{:S(2)}) collective-permute-start(bf16[1024,64]{1,0:T(8,128)(2,1)S(1)} %get-tuple-element.99), channel_id=1, source_target_pairs={{8,0},{16,8},{24,16},{28,24},{20,28},{12,20},{4,12},{0,4},{9,1},{1... | collective-permute-start | bytes 393224 | tf_op jit(solution)/shard_map/ppermute | solution.py:560
  311.0 32.1 %copy-start.13 = (f32[1,256]{1,0:T(1,128)}, f32[1,256]{1,0:T(1,128)S(1)}, u32[]{:S(2)}) copy-start(f32[1,256]{1,0:T(1,128)S(1)} %get-tuple-element.160) | copy-start | bytes 3076
  318.8 9.2 %collective-permute-start.28 = (bf16[1024,64]{1,0:T(8,128)(2,1)S(1)}, bf16[1024,64]{1,0:T(8,128)(2,1)S(1)}, u32[]{:S(2)}, u32[]{:S(2)}) collective-permute-start(bf16[1024,64]{1,0:T(8,128)(2,1)S(1)} %get-tuple-element.106), channel_id=1, source_target_pairs={{0,8},{8,16},{16,24},{24,28},{28,20},{20,12},{12,4},{4,0},{1,9},{9... | collective-permute-start | bytes 393224 | tf_op jit(solution)/shard_map/ppermute | solution.py:559
  319.5 8.5 %collective-permute-start.29 = (bf16[1024,64]{1,0:T(8,128)(2,1)S(1)}, bf16[1024,64]{1,0:T(8,128)(2,1)S(1)}, u32[]{:S(2)}, u32[]{:S(2)}) collective-permute-start(bf16[1024,64]{1,0:T(8,128)(2,1)S(1)} %get-tuple-element.107), channel_id=1, source_target_pairs={{8,0},{16,8},{24,16},{28,24},{20,28},{12,20},{4,12},{0,4},{9,1},{1... | collective-permute-start | bytes 393224 | tf_op jit(solution)/shard_map/ppermute | solution.py:560
  321.7 20.0 %all-to-all-start.5 = ((bf16[32,20,128]{2,1,0:T(8,128)(2,1)}), bf16[32,20,128]{2,1,0:T(8,128)(2,1)S(1)}, u32[]{:S(2)}, u32[]{:S(2)}) async-start(bf16[32,20,128]{2,1,0:T(8,128)(2,1)} %broadcast_in_dim.16), calls=%async_computation.5 | async-start | bytes 393216 | tf_op jit(solution)/shard_map/all_to_all | solution.py:505
  329.2 9.5 %collective-permute-start.30 = (bf16[1024,64]{1,0:T(8,128)(2,1)S(1)}, bf16[1024,64]{1,0:T(8,128)(2,1)S(1)}, u32[]{:S(2)}, u32[]{:S(2)}) collective-permute-start(bf16[1024,64]{1,0:T(8,128)(2,1)S(1)} %get-tuple-element.108), channel_id=1, source_target_pairs={{0,8},{8,16},{16,24},{24,28},{28,20},{20,12},{12,4},{4,0},{1,9},{9... | collective-permute-start | bytes 393224 | tf_op jit(solution)/shard_map/ppermute | solution.py:559
  330.6 9.0 %collective-permute-start.31 = (bf16[1024,64]{1,0:T(8,128)(2,1)S(1)}, bf16[1024,64]{1,0:T(8,128)(2,1)S(1)}, u32[]{:S(2)}, u32[]{:S(2)}) collective-permute-start(bf16[1024,64]{1,0:T(8,128)(2,1)S(1)} %get-tuple-element.109), channel_id=1, source_target_pairs={{8,0},{16,8},{24,16},{28,24},{20,28},{12,20},{4,12},{0,4},{9,1},{1... | collective-permute-start | bytes 393224 | tf_op jit(solution)/shard_map/ppermute | solution.py:560
  (7 other events, 74.0 us)

commit v2 on v0

--- a/solution.py
+++ b/solution.py
@@ -15,7 +15,7 @@
 GROUP = 8
 LINES = 6
 LINE_BYTES = 24 * MIB
-POINTS = 32
+POINTS = 64
 ROWS = 16
 AHEAD = 4
 LOG2E = 1.0 / math.log(2.0)
@@ -70,7 +70,7 @@
     near, block, c = diff_ref.shape
     step_id = pl.program_id(0)
     last = pl.num_programs(0) - 1
-    chunk = 10
+    chunk = near
 
     def project(own_sum, diff_sum):
         weight = w_ref[...].astype(f32)
@@ -609,8 +609,9 @@
     index_two = slot_rows(neighbours_two)
     order_one = by_blocks(index_one, BLOCK).reshape(-1, BLOCK)
     order_two = by_blocks(index_two, BLOCK).reshape(-1, BLOCK)
-    turns_one = by_blocks(index_one, POINTS).reshape(row_count // POINTS, -1)
-    turns_two = by_blocks(index_two, POINTS).reshape(row_count // POINTS, -1)
+    near = neighbours_one.shape[1]
+    turns_one = by_blocks(index_one, POINTS).reshape(-1, near * POINTS)
+    turns_two = by_blocks(index_two, POINTS).reshape(-1, near * POINTS)
 
     diff_one, z_one, stat_one, pivot_one = edge_stats(order_one, table_one, points, weight_one)
     stat_one, order_two, turns_one, turns_two = lax.optimization_barrier(

time: 342 us -> 337 us (0.985)
  Pallas kernels: 153 us -> 148 us
  transfers between devices with their start and end apart: 38 -> 38, of which waited for: 23 -> 24; matrix products, arithmetic and copies ran while one was open for 7% -> 6% of each run, Pallas kernels for 0% -> 0%
where the time goes in v2:
time: 337 us; the launch traced here: 336 us
  Pallas kernels  148 us (44%)
  waiting for transfers between devices  88.3 us (26%)
  starting transfers between devices  64.5 us (19%)
  other arithmetic  14.5 us (4%)
  matrix products  10.4 us (3%)
  local copies, waits for them, and re-layouts  8.87 us (3%)
    pallas_call x2, Pallas kernels, edge_grads(): pl.pallas_call(functools.partial(grads_kernel, float(near * rows), bool(i...  70.4 us
    pallas_call x2, Pallas kernels, edge_stats(): pl.pallas_call(functools.partial(edge_kernel, len(pieces)), grid=(blocks...  44.5 us
    all_to_all x6, starting transfers between devices, exchange(): return lax.all_to_all(shares, BOTH, split_axis=0, concat_axis=0, tiled=True)  39.4 us
    pallas_call x2, Pallas kernels, pool(): pl.pallas_call(functools.partial(pool_kernel, cot is not None, float(near...  33.6 us
    ppermute x6, waiting for transfers between devices, line_table(): behind.append(lax.ppermute(behind[-1], 'pts', onward))  29.2 us
    all_to_all x6, waiting for transfers between devices, exchange(): return lax.all_to_all(shares, BOTH, split_axis=0, concat_axis=0, tiled=True)  28.4 us
    ppermute x6, waiting for transfers between devices, owners_sum(): forth = lax.ppermute(forth, 'pts', onward).astype(f32)  19.7 us
    dot_general x1, matrix products, per_device(): jnp.einsum('kgc,kgd->cd', diff_two, dz_two, preferred_element_type=f32)  7.77 us
  transfers between devices with their start and end apart: 38, of which 24 were waited for; matrix products, arithmetic and copies ran while one was open for 6% of the time, Pallas kernels for 0%

profile of v2, /device:TPU:1, one launch (start us, length us, event | category | flops | bytes accessed | tf_op | source)
XLA Modules:
  0.0 336.2 jit_solution(17460391938759093171)
XLA Ops:
  1.8 2.2 collective-permute-start
  5.4 4.5 %collective-permute-done.refs_2_ = bf16[1024,64]{1,0:T(8,128)(2,1)S(1)} collective-permute-done((bf16[1024,64]{1,0:T(8,128)(2,1)S(1)}, bf16[1024,64]{1,0:T(8,128)(2,1)S(1)}, u32[]{:S(2)}, u32[]{:S(2)}) %collective-permute-start) | collective-permute-done | bytes 131104 | tf_op jit(solution)/shard_map/ppermute | solution.py:527
  9.9 1.2 collective-permute-start.1
  11.5 5.0 %collective-permute-done.1.refs_3_ = bf16[1024,64]{1,0:T(8,128)(2,1)S(1)} collective-permute-done((bf16[1024,64]{1,0:T(8,128)(2,1)S(1)}, bf16[1024,64]{1,0:T(8,128)(2,1)S(1)}, u32[]{:S(2)}, u32[]{:S(2)}) %collective-permute-start.1) | collective-permute-done | bytes 131104 | tf_op jit(solution)/shard_map/ppermute | solution.py:527
  18.0 4.2 %collective-permute-done.2.refs_4_ = bf16[1024,64]{1,0:T(8,128)(2,1)S(1)} collective-permute-done((bf16[1024,64]{1,0:T(8,128)(2,1)S(1)}, bf16[1024,64]{1,0:T(8,128)(2,1)S(1)}, u32[]{:S(2)}, u32[]{:S(2)}) %collective-permute-start.2) | collective-permute-done | bytes 131104 | tf_op jit(solution)/shard_map/ppermute | solution.py:527
  23.7 1.4 fusion.13
  28.0 21.8 %edge_stats.2 = (bf16[20,1024,64]{2,1,0:T(8,128)(2,1)}, f32[20,1024,128]{2,1,0:T(8,128)}, f32[32,2,128]{2,1,0:T(2,128)}, f32[1,128]{1,0:T(1,128)S(1)}) custom-call(s32[160,128]{1,0:T(8,128)S(1)} %reshape.99.refs_0_, bf16[1024,64]{1,0:T(8,128)(2,1)S(1)} %copy.45.refs_1_.refs_10_, bf16[1024,64]{1,0:T(8,128)(2,1)S(1)} %collective-permute-done.refs_2_, ...), custom_call_target="tpu_custom_call" | custom-call | bytes 66000000 | tf_op jit(solution)/shard_map/edge_stats/pallas_call | solution.py:174
  49.7 9.3 %all-to-all-start = ((f32[32,2,128]{2,1,0:T(2,128)}), f32[32,2,128]{2,1,0:T(2,128)S(1)}, u32[]{:S(2)}, u32[]{:S(2)}) async-start(f32[32,2,128]{2,1,0:T(2,128)} %get-tuple-element.64), calls=%async_computation | async-start | bytes 65536 | tf_op jit(solution)/shard_map/all_to_all | solution.py:504
  59.1 7.1 %all-to-all-done.stat_ref = f32[32,2,128]{2,1,0:T(2,128)S(1)} async-done(((f32[32,2,128]{2,1,0:T(2,128)}), f32[32,2,128]{2,1,0:T(2,128)S(1)}, u32[]{:S(2)}, u32[]{:S(2)}) %all-to-all-start) | async-done | bytes 32800 | tf_op jit(solution)/shard_map/all_to_all | solution.py:504
  66.2 12.1 %pool.2 = (bf16[1024,128]{1,0:T(8,128)(2,1)}, f32[20,1024,128]{2,1,0:T(8,128)}, f32[1024,128]{1,0:T(8,128)S(1)}, f32[1024,128]{1,0:T(8,128)S(1)}) custom-call(f32[20,1024,128]{2,1,0:T(8,128)} %get-tuple-element.63.z_ref, f32[32,2,128]{2,1,0:T(2,128)S(1)} %all-to-all-done.stat_ref, f32[1,128]{1,0:T(1,128)S(1)} %get-tuple-element.66.pivot_ref, ...), custom_call_target="tpu_custom_call" | custom-call | bytes 36000000 | tf_op jit(solution)/shard_map/pool/pallas_call | solution.py:296
  78.4 1.5 collective-permute-start.12
  79.8 6.2 %collective-permute-done.8.refs_2_ = bf16[1024,128]{1,0:T(8,128)(2,1)S(1)} collective-permute-done((bf16[1024,128]{1,0:T(8,128)(2,1)}, bf16[1024,128]{1,0:T(8,128)(2,1)S(1)}, u32[]{:S(2)}, u32[]{:S(2)}) %collective-permute-start.8) | collective-permute-done | bytes 262176 | tf_op jit(solution)/shard_map/ppermute | solution.py:527
  86.1 1.5 collective-permute-start.13
  87.5 5.1 %collective-permute-done.9.refs_3_ = bf16[1024,128]{1,0:T(8,128)(2,1)S(1)} collective-permute-done((bf16[1024,128]{1,0:T(8,128)(2,1)S(1)}, bf16[1024,128]{1,0:T(8,128)(2,1)S(1)}, u32[]{:S(2)}, u32[]{:S(2)}) %collective-permute-start.9) | collective-permute-done | bytes 262176 | tf_op jit(solution)/shard_map/ppermute | solution.py:527
  92.6 1.5 collective-permute-start.14
  94.1 4.2 %collective-permute-done.10.refs_4_ = bf16[1024,128]{1,0:T(8,128)(2,1)S(1)} collective-permute-done((bf16[1024,128]{1,0:T(8,128)(2,1)S(1)}, bf16[1024,128]{1,0:T(8,128)(2,1)S(1)}, u32[]{:S(2)}, u32[]{:S(2)}) %collective-permute-start.10) | collective-permute-done | bytes 262176 | tf_op jit(solution)/shard_map/ppermute | solution.py:527
  98.4 1.5 collective-permute-start.15
  99.9 2.3 collective-permute-done.11.refs_5_
  103.2 22.7 %edge_stats.3 = (bf16[20,1024,128]{2,1,0:T(8,128)(2,1)}, f32[20,1024,256]{2,1,0:T(8,128)}, f32[32,2,256]{2,1,0:T(2,128)}, f32[1,256]{1,0:T(1,128)S(1)}) custom-call(s32[160,128]{1,0:T(8,128)S(1)} %reshape.101.refs_0_, bf16[1024,128]{1,0:T(8,128)(2,1)S(1)} %copy-done, bf16[1024,128]{1,0:T(8,128)(2,1)S(1)} %collective-permute-done.8.refs_2_, ...), custom_call_target="tpu_custom_call" | custom-call | bytes 66000000 | tf_op jit(solution)/shard_map/edge_stats/pallas_call | solution.py:174
  126.0 6.6 %all-to-all-start.1 = ((f32[32,2,256]{2,1,0:T(2,128)}), f32[32,2,256]{2,1,0:T(2,128)S(1)}, u32[]{:S(2)}, u32[]{:S(2)}) async-start(f32[32,2,256]{2,1,0:T(2,128)} %get-tuple-element.70), calls=%async_computation.1 | async-start | bytes 131072 | tf_op jit(solution)/shard_map/all_to_all | solution.py:504
  132.6 7.4 %all-to-all-done.1.stat_ref = f32[32,2,256]{2,1,0:T(2,128)S(1)} async-done(((f32[32,2,256]{2,1,0:T(2,128)}), f32[32,2,256]{2,1,0:T(2,128)S(1)}, u32[]{:S(2)}, u32[]{:S(2)}) %all-to-all-start.1) | async-done | bytes 65568 | tf_op jit(solution)/shard_map/all_to_all | solution.py:504
  140.0 21.4 %pool.3 = (bf16[1024,256]{1,0:T(8,128)(2,1)}, f32[20,1024,256]{2,1,0:T(8,128)}, f32[32,2,256]{2,1,0:T(2,128)}) custom-call(f32[20,1024,256]{2,1,0:T(8,128)} %get-tuple-element.69.z_ref, f32[32,2,256]{2,1,0:T(2,128)S(1)} %all-to-all-done.1.stat_ref, f32[1,256]{1,0:T(1,128)S(1)} %get-tuple-element.71.pivot_ref, f32[2,256]{1,0:T(2,128)S(1)} %pad_maximum_fusion.1.norm_ref, ...), custom_call_target="tpu_custom_call" | custom-call | bytes 60000000 | tf_op jit(solution)/shard_map/pool/pallas_call | solution.py:296
  161.5 2.6 all-to-all-start.2
  164.1 7.4 %all-to-all-done.2.grads_ref = f32[32,2,256]{2,1,0:T(2,128)S(1)} async-done(((f32[32,2,256]{2,1,0:T(2,128)}), f32[32,2,256]{2,1,0:T(2,128)S(1)}, u32[]{:S(2)}, u32[]{:S(2)}) %all-to-all-start.2) | async-done | bytes 65568 | tf_op jit(solution)/shard_map/all_to_all | solution.py:504
  171.5 37.3 %edge_grads.2 = (bf16[8192,128]{1,0:T(8,128)(2,1)}, f32[1024,256]{1,0:T(8,128)S(1)}, bf16[20,1024,256]{2,1,0:T(8,128)(2,1)}, bf16[1024,128]{1,0:T(8,128)(2,1)S(1)}) custom-call(s32[16,1280]{1,0:T(8,128)S(1)} %reshape.105.idx_ref, f32[20,1024,256]{2,1,0:T(8,128)} %get-tuple-element.76.slope_ref, f32[20,1024,256]{2,1,0:T(8,128)} %get-tuple-element.69.z_ref, ...), custom_call_target="tpu_custom_call" | custom-call | bytes 105000000 | tf_op jit(solution)/shard_map/edge_grads/pallas_call | solution.py:481
  208.8 1.5 collective-permute-start.17
  211.3 2.2 collective-permute-done.16
  214.7 1.5 collective-permute-start.19
  216.1 5.0 %collective-permute-done.18 = bf16[1024,128]{1,0:T(8,128)(2,1)S(1)} collective-permute-done((bf16[1024,128]{1,0:T(8,128)(2,1)S(1)}, bf16[1024,128]{1,0:T(8,128)(2,1)S(1)}, u32[]{:S(2)}, u32[]{:S(2)}) %collective-permute-start.18) | collective-permute-done | bytes 262176 | tf_op jit(solution)/shard_map/ppermute | solution.py:559
  222.4 1.5 collective-permute-start.21
  223.8 4.1 %collective-permute-done.20 = bf16[1024,128]{1,0:T(8,128)(2,1)S(1)} collective-permute-done((bf16[1024,128]{1,0:T(8,128)(2,1)S(1)}, bf16[1024,128]{1,0:T(8,128)(2,1)S(1)}, u32[]{:S(2)}, u32[]{:S(2)}) %collective-permute-start.20) | collective-permute-done | bytes 262176 | tf_op jit(solution)/shard_map/ppermute | solution.py:559
  228.0 2.0 add_convert_fusion.6
  231.5 3.9 %collective-permute-done.22 = bf16[1024,128]{1,0:T(8,128)(2,1)S(1)} collective-permute-done((bf16[1024,128]{1,0:T(8,128)(2,1)}, bf16[1024,128]{1,0:T(8,128)(2,1)S(1)}, u32[]{:S(2)}, u32[]{:S(2)}) %collective-permute-start.22) | collective-permute-done | bytes 262176 | tf_op jit(solution)/shard_map/ppermute | solution.py:559
  236.1 1.2 convert_add_fusion.1.refs_0_
  238.2 9.2 %all-to-all-start.3 = ((f32[32,2,128]{2,1,0:T(2,128)}), f32[32,2,128]{2,1,0:T(2,128)S(1)}, u32[]{:S(2)}, u32[]{:S(2)}) async-start(f32[32,2,128]{2,1,0:T(2,128)} %broadcast_in_dim.15), calls=%async_computation.3 | async-start | bytes 65536 | tf_op jit(solution)/shard_map/all_to_all | solution.py:504
  247.4 7.8 %fusion = bf16[128,256]{1,0:T(8,128)(2,1)S(1)} fusion(bf16[20,1024,128]{2,1,0:T(8,128)(2,1)} %get-tuple-element.102, bf16[20,1024,256]{2,1,0:T(8,128)(2,1)} %get-tuple-element.103), kind=kOutput, calls=%fused_computation.2 | convolution fusion | flops 1342210048 | bytes 15794176 | tf_op jit(solution)/shard_map/kgc,kgd->cd/dot_general | solution.py:640
  255.8 33.1 %edge_grads.3 = (bf16[8192,64]{1,0:T(8,128)(2,1)}, f32[1024,128]{1,0:T(8,128)S(1)}, f32[64,128]{1,0:T(8,128)S(1)}, bf16[1024,64]{1,0:T(8,128)(2,1)S(1)}) custom-call(s32[16,1280]{1,0:T(8,128)S(1)} %reshape.103.idx_ref, f32[20,1024,128]{2,1,0:T(8,128)} %get-tuple-element.74.slope_ref, f32[20,1024,128]{2,1,0:T(8,128)} %get-tuple-element.63.z_ref, ...), custom_call_target="tpu_custom_call" | custom-call | bytes 105000000 | tf_op jit(solution)/shard_map/edge_grads/pallas_call | solution.py:481
  289.3 1.4 collective-permute-start.24
  291.6 2.4 collective-permute-done.24
  294.0 1.2 collective-permute-done.25
  296.3 1.3 collective-permute-start.26
  298.5 6.4 %all-to-all-start.4 = ((bf16[32,20,128]{2,1,0:T(8,128)(2,1)}), bf16[32,20,128]{2,1,0:T(8,128)(2,1)S(1)}, u32[]{:S(2)}, u32[]{:S(2)}) async-start(bf16[32,20,128]{2,1,0:T(8,128)(2,1)} %reshape.108), calls=%async_computation.4 | async-start | bytes 393216 | tf_op jit(solution)/shard_map/all_to_all | solution.py:504
  306.2 1.4 collective-permute-start.28
  308.3 6.7 %collective-permute-done.28 = bf16[1024,64]{1,0:T(8,128)(2,1)S(1)} collective-permute-done((bf16[1024,64]{1,0:T(8,128)(2,1)S(1)}, bf16[1024,64]{1,0:T(8,128)(2,1)S(1)}, u32[]{:S(2)}, u32[]{:S(2)}) %collective-permute-start.28) | collective-permute-done | bytes 131104 | tf_op jit(solution)/shard_map/ppermute | solution.py:559
  315.0 1.2 collective-permute-done.29
  317.4 2.1 collective-permute-start.30
  320.2 5.2 %all-to-all-start.5 = ((bf16[32,20,128]{2,1,0:T(8,128)(2,1)}), bf16[32,20,128]{2,1,0:T(8,128)(2,1)S(1)}, u32[]{:S(2)}, u32[]{:S(2)}) async-start(bf16[32,20,128]{2,1,0:T(8,128)(2,1)} %broadcast_in_dim.16), calls=%async_computation.5 | async-start | bytes 393216 | tf_op jit(solution)/shard_map/all_to_all | solution.py:504
  328.1 6.5 %all-to-all-done.5 = bf16[32,20,128]{2,1,0:T(8,128)(2,1)S(1)} async-done(((bf16[32,20,128]{2,1,0:T(8,128)(2,1)}), bf16[32,20,128]{2,1,0:T(8,128)(2,1)S(1)}, u32[]{:S(2)}, u32[]{:S(2)}) %all-to-all-start.5) | async-done | bytes 163872 | tf_op jit(solution)/shard_map/all_to_all | solution.py:504
  (135 shorter events, 28.4 us)
Async XLA Ops:
  0.6 58.5 %copy-start.15 = (f32[128]{0:T(128)S(1)}, f32[128]{0:T(128)}, u32[]{:S(2)}) copy-start(f32[128]{0:T(128)} %param.16) | copy-start | bytes 1540
  0.7 58.5 %copy-start.14 = (f32[128]{0:T(128)S(1)}, f32[128]{0:T(128)}, u32[]{:S(2)}) copy-start(f32[128]{0:T(128)} %param.17) | copy-start | bytes 1540
  1.8 8.2 %collective-permute-start = (bf16[1024,64]{1,0:T(8,128)(2,1)S(1)}, bf16[1024,64]{1,0:T(8,128)(2,1)S(1)}, u32[]{:S(2)}, u32[]{:S(2)}) collective-permute-start(bf16[1024,64]{1,0:T(8,128)(2,1)S(1)} %copy.45.refs_1_.refs_10_), channel_id=1, source_target_pairs={{0,8},{8,16},{16,24},{24,28},{28,20},{20,12},{12,4},{4,0},{1,9},{9... | collective-permute-start | bytes 393224 | tf_op jit(solution)/shard_map/ppermute | solution.py:527
  3.9 7.2 %collective-permute-start.4 = (bf16[1024,64]{1,0:T(8,128)(2,1)S(1)}, bf16[1024,64]{1,0:T(8,128)(2,1)S(1)}, u32[]{:S(2)}, u32[]{:S(2)}) collective-permute-start(bf16[1024,64]{1,0:T(8,128)(2,1)S(1)} %copy.45.refs_1_.refs_10_), channel_id=1, source_target_pairs={{8,0},{16,8},{24,16},{28,24},{20,28},{12,20},{4,12},{0,4},{9,1},{1... | collective-permute-start | bytes 393224 | tf_op jit(solution)/shard_map/ppermute | solution.py:528
  9.9 6.6 %collective-permute-start.1 = (bf16[1024,64]{1,0:T(8,128)(2,1)S(1)}, bf16[1024,64]{1,0:T(8,128)(2,1)S(1)}, u32[]{:S(2)}, u32[]{:S(2)}) collective-permute-start(bf16[1024,64]{1,0:T(8,128)(2,1)S(1)} %collective-permute-done.refs_2_), channel_id=1, source_target_pairs={{0,8},{8,16},{16,24},{24,28},{28,20},{20,12},{12,4},{4,0},{1,9},{9... | collective-permute-start | bytes 393224 | tf_op jit(solution)/shard_map/ppermute | solution.py:527
  11.1 6.3 %collective-permute-start.5 = (bf16[1024,64]{1,0:T(8,128)(2,1)S(1)}, bf16[1024,64]{1,0:T(8,128)(2,1)S(1)}, u32[]{:S(2)}, u32[]{:S(2)}) collective-permute-start(bf16[1024,64]{1,0:T(8,128)(2,1)S(1)} %collective-permute-done.4.refs_9_), channel_id=1, source_target_pairs={{8,0},{16,8},{24,16},{28,24},{20,28},{12,20},{4,12},{0,4},{9,1},{1... | collective-permute-start | bytes 393224 | tf_op jit(solution)/shard_map/ppermute | solution.py:528
  16.5 5.6 %collective-permute-start.2 = (bf16[1024,64]{1,0:T(8,128)(2,1)S(1)}, bf16[1024,64]{1,0:T(8,128)(2,1)S(1)}, u32[]{:S(2)}, u32[]{:S(2)}) collective-permute-start(bf16[1024,64]{1,0:T(8,128)(2,1)S(1)} %collective-permute-done.1.refs_3_), channel_id=1, source_target_pairs={{0,8},{8,16},{16,24},{24,28},{28,20},{20,12},{12,4},{4,0},{1,9},{9... | collective-permute-start | bytes 393224 | tf_op jit(solution)/shard_map/ppermute | solution.py:527
  17.4 5.5 %collective-permute-start.6 = (bf16[1024,64]{1,0:T(8,128)(2,1)S(1)}, bf16[1024,64]{1,0:T(8,128)(2,1)S(1)}, u32[]{:S(2)}, u32[]{:S(2)}) collective-permute-start(bf16[1024,64]{1,0:T(8,128)(2,1)S(1)} %collective-permute-done.5.refs_8_), channel_id=1, source_target_pairs={{8,0},{16,8},{24,16},{28,24},{20,28},{12,20},{4,12},{0,4},{9,1},{1... | collective-permute-start | bytes 393224 | tf_op jit(solution)/shard_map/ppermute | solution.py:528
  22.1 4.2 %collective-permute-start.3 = (bf16[512,64]{1,0:T(8,128)(2,1)S(1)}, bf16[512,64]{1,0:T(8,128)(2,1)S(1)}, u32[]{:S(2)}, u32[]{:S(2)}) collective-permute-start(bf16[512,64]{1,0:T(8,128)(2,1)S(1)} %slice.138), channel_id=1, source_target_pairs={{0,8},{8,16},{16,24},{24,28},{28,20},{20,12},{12,4},{4,0},{1,9},{9... | collective-permute-start | bytes 196616 | tf_op jit(solution)/shard_map/ppermute | solution.py:530
  22.9 4.3 %collective-permute-start.7 = (bf16[512,64]{1,0:T(8,128)(2,1)S(1)}, bf16[512,64]{1,0:T(8,128)(2,1)S(1)}, u32[]{:S(2)}, u32[]{:S(2)}) collective-permute-start(bf16[512,64]{1,0:T(8,128)(2,1)S(1)} %slice.139), channel_id=1, source_target_pairs={{8,0},{16,8},{24,16},{28,24},{20,28},{12,20},{4,12},{0,4},{9,1},{1... | collective-permute-start | bytes 196616 | tf_op jit(solution)/shard_map/ppermute | solution.py:531
  49.7 16.5 %all-to-all-start = ((f32[32,2,128]{2,1,0:T(2,128)}), f32[32,2,128]{2,1,0:T(2,128)S(1)}, u32[]{:S(2)}, u32[]{:S(2)}) async-start(f32[32,2,128]{2,1,0:T(2,128)} %get-tuple-element.64), calls=%async_computation | async-start | bytes 65536 | tf_op jit(solution)/shard_map/all_to_all | solution.py:504
  66.2 36.1 %copy-start.2 = (bf16[256,256]{1,0:T(8,128)(2,1)S(1)}, bf16[256,256]{1,0:T(8,128)(2,1)}, u32[]{:S(2)}) copy-start(bf16[256,256]{1,0:T(8,128)(2,1)} %refs_11_.3) | copy-start | bytes 393220
  66.2 66.4 %copy-start.11 = (f32[256]{0:T(256)S(1)}, f32[256]{0:T(256)}, u32[]{:S(2)}) copy-start(f32[256]{0:T(256)} %param.20) | copy-start | bytes 3076
  66.2 66.4 %copy-start.12 = (f32[256]{0:T(256)S(1)}, f32[256]{0:T(256)}, u32[]{:S(2)}) copy-start(f32[256]{0:T(256)} %param.19) | copy-start | bytes 3076
  66.2 73.8 %copy-start.3 = (bf16[1024,256]{1,0:T(8,128)(2,1)S(1)}, bf16[1024,256]{1,0:T(8,128)(2,1)}, u32[]{:S(2)}) copy-start(bf16[1024,256]{1,0:T(8,128)(2,1)} %refs_0_.1) | copy-start | bytes 1572868
  78.4 7.7 %collective-permute-start.8 = (bf16[1024,128]{1,0:T(8,128)(2,1)}, bf16[1024,128]{1,0:T(8,128)(2,1)S(1)}, u32[]{:S(2)}, u32[]{:S(2)}) collective-permute-start(bf16[1024,128]{1,0:T(8,128)(2,1)} %get-tuple-element.135.refs_1_.refs_10_), channel_id=1, source_target_pairs={{0,8},{8,16},{16,24},{24,28},{28,20},{20,12},{12,4},{4,0},{1,9},{9... | collective-permute-start | bytes 786440 | tf_op jit(solution)/shard_map/ppermute | solution.py:527
  78.4 7.7 %collective-permute-start.12 = (bf16[1024,128]{1,0:T(8,128)(2,1)}, bf16[1024,128]{1,0:T(8,128)(2,1)S(1)}, u32[]{:S(2)}, u32[]{:S(2)}) collective-permute-start(bf16[1024,128]{1,0:T(8,128)(2,1)} %get-tuple-element.135.refs_1_.refs_10_), channel_id=1, source_target_pairs={{8,0},{16,8},{24,16},{28,24},{20,28},{12,20},{4,12},{0,4},{9,1},{1... | collective-permute-start | bytes 786440 | tf_op jit(solution)/shard_map/ppermute | solution.py:528
  86.1 6.6 %collective-permute-start.9 = (bf16[1024,128]{1,0:T(8,128)(2,1)S(1)}, bf16[1024,128]{1,0:T(8,128)(2,1)S(1)}, u32[]{:S(2)}, u32[]{:S(2)}) collective-permute-start(bf16[1024,128]{1,0:T(8,128)(2,1)S(1)} %collective-permute-done.8.refs_2_), channel_id=1, source_target_pairs={{0,8},{8,16},{16,24},{24,28},{28,20},{20,12},{12,4},{4,0},{1,9},{9... | collective-permute-start | bytes 786440 | tf_op jit(solution)/shard_map/ppermute | solution.py:527
  86.1 6.6 %collective-permute-start.13 = (bf16[1024,128]{1,0:T(8,128)(2,1)S(1)}, bf16[1024,128]{1,0:T(8,128)(2,1)S(1)}, u32[]{:S(2)}, u32[]{:S(2)}) collective-permute-start(bf16[1024,128]{1,0:T(8,128)(2,1)S(1)} %collective-permute-done.12.refs_9_), channel_id=1, source_target_pairs={{8,0},{16,8},{24,16},{28,24},{20,28},{12,20},{4,12},{0,4},{9,1},{1... | collective-permute-start | bytes 786440 | tf_op jit(solution)/shard_map/ppermute | solution.py:528
  92.6 5.6 %collective-permute-start.10 = (bf16[1024,128]{1,0:T(8,128)(2,1)S(1)}, bf16[1024,128]{1,0:T(8,128)(2,1)S(1)}, u32[]{:S(2)}, u32[]{:S(2)}) collective-permute-start(bf16[1024,128]{1,0:T(8,128)(2,1)S(1)} %collective-permute-done.9.refs_3_), channel_id=1, source_target_pairs={{0,8},{8,16},{16,24},{24,28},{28,20},{20,12},{12,4},{4,0},{1,9},{9... | collective-permute-start | bytes 786440 | tf_op jit(solution)/shard_map/ppermute | solution.py:527
  92.6 5.7 %collective-permute-start.14 = (bf16[1024,128]{1,0:T(8,128)(2,1)S(1)}, bf16[1024,128]{1,0:T(8,128)(2,1)S(1)}, u32[]{:S(2)}, u32[]{:S(2)}) collective-permute-start(bf16[1024,128]{1,0:T(8,128)(2,1)S(1)} %collective-permute-done.13.refs_8_), channel_id=1, source_target_pairs={{8,0},{16,8},{24,16},{28,24},{20,28},{12,20},{4,12},{0,4},{9,1},{1... | collective-permute-start | bytes 786440 | tf_op jit(solution)/shard_map/ppermute | solution.py:528
  98.3 3.9 %collective-permute-start.11 = (bf16[512,128]{1,0:T(8,128)(2,1)S(1)}, bf16[512,128]{1,0:T(8,128)(2,1)S(1)}, u32[]{:S(2)}, u32[]{:S(2)}) collective-permute-start(bf16[512,128]{1,0:T(8,128)(2,1)S(1)} %slice.140), channel_id=1, source_target_pairs={{0,8},{8,16},{16,24},{24,28},{28,20},{20,12},{12,4},{4,0},{1,9},{9... | collective-permute-start | bytes 393224 | tf_op jit(solution)/shard_map/ppermute | solution.py:530
  98.4 3.9 %collective-permute-start.15 = (bf16[512,128]{1,0:T(8,128)(2,1)S(1)}, bf16[512,128]{1,0:T(8,128)(2,1)S(1)}, u32[]{:S(2)}, u32[]{:S(2)}) collective-permute-start(bf16[512,128]{1,0:T(8,128)(2,1)S(1)} %slice.141), channel_id=1, source_target_pairs={{8,0},{16,8},{24,16},{28,24},{20,28},{12,20},{4,12},{0,4},{9,1},{1... | collective-permute-start | bytes 393224 | tf_op jit(solution)/shard_map/ppermute | solution.py:531
  126.0 14.1 %all-to-all-start.1 = ((f32[32,2,256]{2,1,0:T(2,128)}), f32[32,2,256]{2,1,0:T(2,128)S(1)}, u32[]{:S(2)}, u32[]{:S(2)}) async-start(f32[32,2,256]{2,1,0:T(2,128)} %get-tuple-element.70), calls=%async_computation.1 | async-start | bytes 131072 | tf_op jit(solution)/shard_map/all_to_all | solution.py:504
  161.5 10.0 %all-to-all-start.2 = ((f32[32,2,256]{2,1,0:T(2,128)}), f32[32,2,256]{2,1,0:T(2,128)S(1)}, u32[]{:S(2)}, u32[]{:S(2)}) async-start(f32[32,2,256]{2,1,0:T(2,128)} %get-tuple-element.77), calls=%async_computation.2 | async-start | bytes 131072 | tf_op jit(solution)/shard_map/all_to_all | solution.py:504
  208.7 22.7 %copy-start.5 = (bf16[128,128]{1,0:T(8,128)(2,1)S(1)}, bf16[128,128]{1,0:T(8,128)(2,1)}, u32[]{:S(2)}) copy-start(bf16[128,128]{1,0:T(8,128)(2,1)} %refs_11_.2) | copy-start | bytes 98308
  208.7 22.7 %slice-start = ((bf16[128,128]{1,0:T(8,128)(2,1)}), bf16[64,128]{1,0:T(8,128)(2,1)S(1)}, s32[]{:S(2)}) async-start(bf16[128,128]{1,0:T(8,128)(2,1)} %refs_11_.2), calls=%async_computation.6 | async-start | bytes 32768 | tf_op jit(solution)/shard_map/slice | solution.py:448
  208.7 4.7 %collective-permute-start.16 = (bf16[512,128]{1,0:T(8,128)(2,1)S(1)}, bf16[512,128]{1,0:T(8,128)(2,1)S(1)}, u32[]{:S(2)}, u32[]{:S(2)}) collective-permute-start(bf16[512,128]{1,0:T(8,128)(2,1)S(1)} %get-tuple-element.163), channel_id=1, source_target_pairs={{0,8},{8,16},{16,24},{24,28},{28,20},{20,12},{12,4},{4,0},{1,9},{9... | collective-permute-start | bytes 393224 | tf_op jit(solution)/shard_map/ppermute | solution.py:545
  208.8 4.7 %collective-permute-start.17 = (bf16[512,128]{1,0:T(8,128)(2,1)S(1)}, bf16[512,128]{1,0:T(8,128)(2,1)S(1)}, u32[]{:S(2)}, u32[]{:S(2)}) collective-permute-start(bf16[512,128]{1,0:T(8,128)(2,1)S(1)} %get-tuple-element.162), channel_id=1, source_target_pairs={{8,0},{16,8},{24,16},{28,24},{20,28},{12,20},{4,12},{0,4},{9,1},{1... | collective-permute-start | bytes 393224 | tf_op jit(solution)/shard_map/ppermute | solution.py:546
  214.6 6.6 %collective-permute-start.18 = (bf16[1024,128]{1,0:T(8,128)(2,1)S(1)}, bf16[1024,128]{1,0:T(8,128)(2,1)S(1)}, u32[]{:S(2)}, u32[]{:S(2)}) collective-permute-start(bf16[1024,128]{1,0:T(8,128)(2,1)S(1)} %get-tuple-element.84), channel_id=1, source_target_pairs={{0,8},{8,16},{16,24},{24,28},{28,20},{20,12},{12,4},{4,0},{1,9},{9... | collective-permute-start | bytes 786440 | tf_op jit(solution)/shard_map/ppermute | solution.py:559
  214.7 6.5 %collective-permute-start.19 = (bf16[1024,128]{1,0:T(8,128)(2,1)S(1)}, bf16[1024,128]{1,0:T(8,128)(2,1)S(1)}, u32[]{:S(2)}, u32[]{:S(2)}) collective-permute-start(bf16[1024,128]{1,0:T(8,128)(2,1)S(1)} %get-tuple-element.85), channel_id=1, source_target_pairs={{8,0},{16,8},{24,16},{28,24},{20,28},{12,20},{4,12},{0,4},{9,1},{1... | collective-permute-start | bytes 786440 | tf_op jit(solution)/shard_map/ppermute | solution.py:560
  222.3 5.6 %collective-permute-start.20 = (bf16[1024,128]{1,0:T(8,128)(2,1)S(1)}, bf16[1024,128]{1,0:T(8,128)(2,1)S(1)}, u32[]{:S(2)}, u32[]{:S(2)}) collective-permute-start(bf16[1024,128]{1,0:T(8,128)(2,1)S(1)} %get-tuple-element.86), channel_id=1, source_target_pairs={{0,8},{8,16},{16,24},{24,28},{28,20},{20,12},{12,4},{4,0},{1,9},{9... | collective-permute-start | bytes 786440 | tf_op jit(solution)/shard_map/ppermute | solution.py:559
  222.4 5.6 %collective-permute-start.21 = (bf16[1024,128]{1,0:T(8,128)(2,1)S(1)}, bf16[1024,128]{1,0:T(8,128)(2,1)S(1)}, u32[]{:S(2)}, u32[]{:S(2)}) collective-permute-start(bf16[1024,128]{1,0:T(8,128)(2,1)S(1)} %get-tuple-element.87), channel_id=1, source_target_pairs={{8,0},{16,8},{24,16},{28,24},{20,28},{12,20},{4,12},{0,4},{9,1},{1... | collective-permute-start | bytes 786440 | tf_op jit(solution)/shard_map/ppermute | solution.py:560
  229.9 5.4 %collective-permute-start.22 = (bf16[1024,128]{1,0:T(8,128)(2,1)}, bf16[1024,128]{1,0:T(8,128)(2,1)S(1)}, u32[]{:S(2)}, u32[]{:S(2)}) collective-permute-start(bf16[1024,128]{1,0:T(8,128)(2,1)} %get-tuple-element.88), channel_id=1, source_target_pairs={{0,8},{8,16},{16,24},{24,28},{28,20},{20,12},{12,4},{4,0},{1,9},{9... | collective-permute-start | bytes 786440 | tf_op jit(solution)/shard_map/ppermute | solution.py:559
  230.3 5.8 %collective-permute-start.23 = (bf16[1024,128]{1,0:T(8,128)(2,1)}, bf16[1024,128]{1,0:T(8,128)(2,1)}, u32[]{:S(2)}, u32[]{:S(2)}) collective-permute-start(bf16[1024,128]{1,0:T(8,128)(2,1)} %get-tuple-element.89), channel_id=1, source_target_pairs={{8,0},{16,8},{24,16},{28,24},{20,28},{12,20},{4,12},{0,4},{9,1},{1... | collective-permute-start | bytes 786440 | tf_op jit(solution)/shard_map/ppermute | solution.py:560
  238.2 17.7 %all-to-all-start.3 = ((f32[32,2,128]{2,1,0:T(2,128)}), f32[32,2,128]{2,1,0:T(2,128)S(1)}, u32[]{:S(2)}, u32[]{:S(2)}) async-start(f32[32,2,128]{2,1,0:T(2,128)} %broadcast_in_dim.15), calls=%async_computation.3 | async-start | bytes 65536 | tf_op jit(solution)/shard_map/all_to_all | solution.py:504
  255.8 33.2 %copy-start.6 = (bf16[1024,64]{0,1:T(8,128)(2,1)S(1)}, bf16[1024,64]{0,1:T(8,128)(2,1)}, u32[]{:S(2)}) copy-start(bf16[1024,64]{0,1:T(8,128)(2,1)} %param.11) | copy-start | bytes 393220
  289.3 4.7 %collective-permute-start.24 = (bf16[512,64]{1,0:T(8,128)(2,1)S(1)}, bf16[512,64]{1,0:T(8,128)(2,1)S(1)}, u32[]{:S(2)}, u32[]{:S(2)}) collective-permute-start(bf16[512,64]{1,0:T(8,128)(2,1)S(1)} %get-tuple-element.161), channel_id=1, source_target_pairs={{0,8},{8,16},{16,24},{24,28},{28,20},{20,12},{12,4},{4,0},{1,9},{9... | collective-permute-start | bytes 196616 | tf_op jit(solution)/shard_map/ppermute | solution.py:545
  290.8 4.4 %collective-permute-start.25 = (bf16[512,64]{1,0:T(8,128)(2,1)S(1)}, bf16[512,64]{1,0:T(8,128)(2,1)S(1)}, u32[]{:S(2)}, u32[]{:S(2)}) collective-permute-start(bf16[512,64]{1,0:T(8,128)(2,1)S(1)} %get-tuple-element.160), channel_id=1, source_target_pairs={{8,0},{16,8},{24,16},{28,24},{20,28},{12,20},{4,12},{0,4},{9,1},{1... | collective-permute-start | bytes 196616 | tf_op jit(solution)/shard_map/ppermute | solution.py:546
  296.3 8.7 %collective-permute-start.26 = (bf16[1024,64]{1,0:T(8,128)(2,1)S(1)}, bf16[1024,64]{1,0:T(8,128)(2,1)S(1)}, u32[]{:S(2)}, u32[]{:S(2)}) collective-permute-start(bf16[1024,64]{1,0:T(8,128)(2,1)S(1)} %get-tuple-element.107), channel_id=1, source_target_pairs={{0,8},{8,16},{16,24},{24,28},{28,20},{20,12},{12,4},{4,0},{1,9},{9... | collective-permute-start | bytes 393224 | tf_op jit(solution)/shard_map/ppermute | solution.py:559
  297.5 7.4 %collective-permute-start.27 = (bf16[1024,64]{1,0:T(8,128)(2,1)S(1)}, bf16[1024,64]{1,0:T(8,128)(2,1)S(1)}, u32[]{:S(2)}, u32[]{:S(2)}) collective-permute-start(bf16[1024,64]{1,0:T(8,128)(2,1)S(1)} %get-tuple-element.108), channel_id=1, source_target_pairs={{8,0},{16,8},{24,16},{28,24},{20,28},{12,20},{4,12},{0,4},{9,1},{1... | collective-permute-start | bytes 393224 | tf_op jit(solution)/shard_map/ppermute | solution.py:560
  297.8 38.3 %copy-start.13 = (f32[1,256]{1,0:T(1,128)}, f32[1,256]{1,0:T(1,128)S(1)}, u32[]{:S(2)}) copy-start(f32[1,256]{1,0:T(1,128)S(1)} %get-tuple-element.166) | copy-start | bytes 3076
  298.5 18.8 %all-to-all-start.4 = ((bf16[32,20,128]{2,1,0:T(8,128)(2,1)}), bf16[32,20,128]{2,1,0:T(8,128)(2,1)S(1)}, u32[]{:S(2)}, u32[]{:S(2)}) async-start(bf16[32,20,128]{2,1,0:T(8,128)(2,1)} %reshape.108), calls=%async_computation.4 | async-start | bytes 393216 | tf_op jit(solution)/shard_map/all_to_all | solution.py:504
  306.2 8.8 %collective-permute-start.28 = (bf16[1024,64]{1,0:T(8,128)(2,1)S(1)}, bf16[1024,64]{1,0:T(8,128)(2,1)S(1)}, u32[]{:S(2)}, u32[]{:S(2)}) collective-permute-start(bf16[1024,64]{1,0:T(8,128)(2,1)S(1)} %get-tuple-element.109), channel_id=1, source_target_pairs={{0,8},{8,16},{16,24},{24,28},{28,20},{20,12},{12,4},{4,0},{1,9},{9... | collective-permute-start | bytes 393224 | tf_op jit(solution)/shard_map/ppermute | solution.py:559
  307.6 8.6 %collective-permute-start.29 = (bf16[1024,64]{1,0:T(8,128)(2,1)S(1)}, bf16[1024,64]{1,0:T(8,128)(2,1)S(1)}, u32[]{:S(2)}, u32[]{:S(2)}) collective-permute-start(bf16[1024,64]{1,0:T(8,128)(2,1)S(1)} %get-tuple-element.110), channel_id=1, source_target_pairs={{8,0},{16,8},{24,16},{28,24},{20,28},{12,20},{4,12},{0,4},{9,1},{1... | collective-permute-start | bytes 393224 | tf_op jit(solution)/shard_map/ppermute | solution.py:560
  317.4 8.8 %collective-permute-start.30 = (bf16[1024,64]{1,0:T(8,128)(2,1)S(1)}, bf16[1024,64]{1,0:T(8,128)(2,1)S(1)}, u32[]{:S(2)}, u32[]{:S(2)}) collective-permute-start(bf16[1024,64]{1,0:T(8,128)(2,1)S(1)} %get-tuple-element.114), channel_id=1, source_target_pairs={{0,8},{8,16},{16,24},{24,28},{28,20},{20,12},{12,4},{4,0},{1,9},{9... | collective-permute-start | bytes 393224 | tf_op jit(solution)/shard_map/ppermute | solution.py:559
  319.5 6.7 %collective-permute-start.31 = (bf16[1024,64]{1,0:T(8,128)(2,1)S(1)}, bf16[1024,64]{1,0:T(8,128)(2,1)S(1)}, u32[]{:S(2)}, u32[]{:S(2)}) collective-permute-start(bf16[1024,64]{1,0:T(8,128)(2,1)S(1)} %get-tuple-element.115), channel_id=1, source_target_pairs={{8,0},{16,8},{24,16},{28,24},{20,28},{12,20},{4,12},{0,4},{9,1},{1... | collective-permute-start | bytes 393224 | tf_op jit(solution)/shard_map/ppermute | solution.py:560
  320.2 14.4 %all-to-all-start.5 = ((bf16[32,20,128]{2,1,0:T(8,128)(2,1)}), bf16[32,20,128]{2,1,0:T(8,128)(2,1)S(1)}, u32[]{:S(2)}, u32[]{:S(2)}) async-start(bf16[32,20,128]{2,1,0:T(8,128)(2,1)} %broadcast_in_dim.16), calls=%async_computation.5 | async-start | bytes 393216 | tf_op jit(solution)/shard_map/all_to_all | solution.py:504
  (7 other events, 52.1 us)
